TPU v7x, 32 devices: a whole 2x2x4 slice. The times are simulated.
32 devices in a mesh: crop: 2 (over x), row: 4 (over y, core), col: 4 (over z).
Axes of the slice: x: 2, y: 2, z: 4, core: 2. Of those that a mesh axis runs over, the one named last changes fastest.
Arguments:
- alignment_activations: bfloat16 [128, 256, 256], P('crop', 'row'), parts along dimension 0, may hold values from -12 to 12
- sequence_presence_flags: int32 [128, 256], P('crop'), parts along dimension 0, may hold values 0 or 1
- residue_padding_mask: int32 [512], P('crop'), parts along dimension 0, may hold values 0 or 1
- left_weight: bfloat16 [256, 32], replicated, may hold values from -0.375 to 0.375
- right_weight: bfloat16 [256, 32], replicated, may hold values from -0.375 to 0.375
- output_weight: bfloat16 [1024, 128], replicated, may hold values from -0.1875 to 0.1875
- cotangent: bfloat16 [512, 256, 128], P(('crop', 'row'), 'col'), parts along dimension 0, may hold values from -6 to 6
Outputs:
- pair_state_update: bfloat16 [512, 256, 128], P(('crop', 'row'), 'col'), parts along dimension 0
- alignment_gradient: bfloat16 [128, 256, 256], P('crop', 'row'), parts along dimension 0
- grad_w_out: float32 [2048, 128], P(('crop', 'row', 'col')), parts along dimension 0
- left_weight_gradient: float32 [512, 32], P('crop'), parts along dimension 0
- right_weight_gradient: float32 [512, 32], P('crop'), parts along dimension 0
There are 2 independent parts, one for each index of `crop`. A program takes and returns all parts, laid end to end along the dimension named above; an argument that names none is the same for every part. Nothing has to cross between parts.
All inputs are finite; a program needn't handle non-finite values.
Results may differ from a plain program's by a relative error of at most 0.0075.
Values may be sent and summed in bfloat16 or wider, within the bound.
A program may use at most 128 MiB of HBM per device.

v0:
```python
import math

import jax
import jax.numpy as jnp
from jax import lax
from jax.sharding import PartitionSpec as P

norm_eps = 1e-05


def broadcast(value, axis, root):
    mine = lax.axis_index(axis) == root
    return lax.psum(jnp.where(mine, value, jnp.zeros_like(value)), axis)


def layer_normalize(values):
    floats = values.astype(jnp.float32)
    average = jnp.mean(floats, -1, keepdims=True)
    centred = floats - average
    variance = jnp.mean(centred * centred, -1, keepdims=True)
    inverse_deviation = lax.rsqrt(variance + norm_eps)
    return (centred * inverse_deviation, inverse_deviation)


def body(
    alignment_activations,
    sequence_presence_flags,
    residue_padding_mask,
    left_weight,
    right_weight,
    output_weight,
    cotangent,
):
    row_idx = lax.axis_index("row")
    col_idx = lax.axis_index("col")
    row_devs = lax.axis_size("row")
    col_devs = lax.axis_size("col")
    block_ratio = row_devs // col_devs
    sample_draws = alignment_activations.shape[0]
    local_residues = alignment_activations.shape[1]
    residue_total = sequence_presence_flags.shape[1]
    col_len = residue_total // col_devs
    hidden_width = left_weight.shape[1]
    active_mask = (sequence_presence_flags * residue_padding_mask[None, :]).astype(jnp.float32)
    own_live = lax.dynamic_slice_in_dim(active_mask, row_idx * local_residues, local_residues, 1)
    unit_alignment, inverse_deviation = layer_normalize(alignment_activations)
    normalized_input = unit_alignment.astype(jnp.bfloat16)
    left_rows = (
        jnp.einsum("snd,dc->snc", normalized_input, left_weight, preferred_element_type=jnp.float32)
        * own_live[..., None]
    ).astype(jnp.bfloat16)
    right_own = (
        jnp.einsum(
            "snd,dc->snc", normalized_input, right_weight, preferred_element_type=jnp.float32
        )
        * own_live[..., None]
    ).astype(jnp.bfloat16)
    every_right = lax.all_gather(right_own, "row", axis=1, tiled=True)
    right_cols = lax.dynamic_slice_in_dim(every_right, col_idx * col_len, col_len, 1)
    live_cols = lax.dynamic_slice_in_dim(active_mask, col_idx * col_len, col_len, 1)
    pair_count = jnp.dot(own_live.T, live_cols, precision=lax.Precision.HIGHEST)
    divisor = jnp.maximum(pair_count, 1.0)
    block_rows = math.gcd(local_residues, 16)
    output_gradient = jnp.zeros((hidden_width * hidden_width, output_weight.shape[1]), jnp.float32)
    right_acc = jnp.zeros((sample_draws, col_len, hidden_width), jnp.float32)
    pieces_pair = []
    pieces_left = []
    for first_row in range(0, local_residues, block_rows):
        left_block = left_rows[:, first_row : first_row + block_rows]
        block_div = divisor[first_row : first_row + block_rows][..., None]
        outer_prod = jnp.einsum(
            "sic,sje->ijce", left_block, right_cols, preferred_element_type=jnp.float32
        ).astype(jnp.bfloat16)
        outer_prod = outer_prod.reshape(block_rows, col_len, hidden_width * hidden_width)
        pair_block = (
            jnp.einsum("ijk,kz->ijz", outer_prod, output_weight, preferred_element_type=jnp.float32)
            / block_div
        )
        pieces_pair.append(pair_block.astype(jnp.bfloat16))
        scaled = (
            cotangent[first_row : first_row + block_rows].astype(jnp.float32) / block_div
        ).astype(jnp.bfloat16)
        output_gradient = output_gradient + jnp.einsum(
            "ijk,ijz->kz", outer_prod, scaled, preferred_element_type=jnp.float32
        )
        grad_outer = jnp.einsum(
            "ijz,kz->ijk", scaled, output_weight, preferred_element_type=jnp.float32
        ).astype(jnp.bfloat16)
        grad_outer = grad_outer.reshape(block_rows, col_len, hidden_width, hidden_width)
        pieces_left.append(
            jnp.einsum("ijce,sje->sic", grad_outer, right_cols, preferred_element_type=jnp.float32)
        )
        right_acc = right_acc + jnp.einsum(
            "ijce,sic->sje", grad_outer, left_block, preferred_element_type=jnp.float32
        )
    pair_state_update = jnp.concatenate(pieces_pair, 0)
    left_part = jnp.concatenate(pieces_left, 1)
    left_total = lax.psum(left_part, "col")
    grad_left = (left_total * own_live[..., None]).astype(jnp.bfloat16)
    right_full = lax.psum(right_acc, "row")
    offer = lax.dynamic_slice_in_dim(
        right_full, row_idx % block_ratio * local_residues, local_residues, 1
    )
    offer = (offer * own_live[..., None]).astype(jnp.bfloat16)
    grad_right = broadcast(offer, "col", row_idx // block_ratio)
    left_wgrad = jnp.einsum(
        "snd,snc->dc", normalized_input, grad_left, preferred_element_type=jnp.float32
    )
    right_wgrad = jnp.einsum(
        "snd,snc->dc", normalized_input, grad_right, preferred_element_type=jnp.float32
    )
    first_factor_accrued, right_sum = lax.psum((left_wgrad, right_wgrad), "row")
    out_share = lax.psum_scatter(output_gradient, ("row", "col"), scatter_dimension=0, tiled=True)
    normalized_gradient = jnp.einsum(
        "snc,dc->snd", grad_left, left_weight, preferred_element_type=jnp.float32
    )
    normalized_gradient = normalized_gradient + jnp.einsum(
        "snc,dc->snd", grad_right, right_weight, preferred_element_type=jnp.float32
    )
    centered_gradient = (
        normalized_gradient
        - jnp.mean(normalized_gradient, -1, keepdims=True)
        - unit_alignment * jnp.mean(normalized_gradient * unit_alignment, -1, keepdims=True)
    )
    alignment_gradient = (inverse_deviation * centered_gradient).astype(jnp.bfloat16)
    return (
        pair_state_update,
        alignment_gradient,
        out_share / residue_total,
        first_factor_accrued / residue_total,
        right_sum / residue_total,
    )


def solution(mesh):
    return jax.shard_map(
        body,
        mesh=mesh,
        in_specs=(
            P("crop", "row", None),
            P("crop", None),
            P("crop"),
            P(),
            P(),
            P(),
            P(("crop", "row"), "col", None),
        ),
        out_specs=(
            P(("crop", "row"), "col", None),
            P("crop", "row", None),
            P(("crop", "row", "col"), None),
            P("crop", None),
            P("crop", None),
        ),
        check_vma=False,
    )
```

profile of v0, /device:TPU:0, one launch (start us, length us, event | category | flops | bytes accessed | tf_op | source)
XLA Modules:
  0.0 375.1 jit_solution(1101399196147577670)
XLA Ops:
  9.7 2.5 fusion.9
  22.4 3.1 convolution_convert_fusion.3
  25.5 4.7 %copy.114 = bf16[16,64,1024]{1,2,0:T(8,128)(2,1)} copy(bf16[16,64,1024]{2,1,0:T(8,128)(2,1)} %convolution_convert_fusion.3) | data formatting | bytes 4194304 | tf_op jit(solution)/shard_map/convert_element_type | solution.py:88
  30.3 3.0 convolution_convert_fusion
  33.3 4.9 %copy.120 = bf16[16,64,1024]{1,2,0:T(8,128)(2,1)} copy(bf16[16,64,1024]{2,1,0:T(8,128)(2,1)} %convolution_convert_fusion) | data formatting | bytes 4194304 | tf_op jit(solution)/shard_map/convert_element_type | solution.py:88
  38.2 3.0 convolution_convert_fusion.1
  41.3 4.8 %copy.118 = bf16[16,64,1024]{1,2,0:T(8,128)(2,1)} copy(bf16[16,64,1024]{2,1,0:T(8,128)(2,1)} %convolution_convert_fusion.1) | data formatting | bytes 4194304 | tf_op jit(solution)/shard_map/convert_element_type | solution.py:88
  46.1 3.0 convolution_convert_fusion.2
  49.1 5.2 %copy.116 = bf16[16,64,1024]{1,2,0:T(8,128)(2,1)} copy(bf16[16,64,1024]{2,1,0:T(8,128)(2,1)} %convolution_convert_fusion.2) | data formatting | bytes 4194304 | tf_op jit(solution)/shard_map/convert_element_type | solution.py:88
  54.4 3.8 %fusion.26 = f32[64,64,32]{1,0,2:T(8,128)S(1)} fusion(bf16[16,64,32,32]{1,3,2,0:T(8,128)(2,1)} %bitcast.141, bf16[64,16,32]{0,2,1:T(8,128)(2,1)S(1)} %copy.102), kind=kOutput, calls=%fused_computation.37 | convolution fusion | flops 134217728 | bytes 2686976 | tf_op jit(solution)/shard_map/ijce,sic->sje/dot_general | solution.py:93
  62.6 3.2 copy_add_fusion
  65.9 38.9 %all-reduce.8.cloned.1.call-done = f32[64,64,32]{1,2,0:T(8,128)} async-done(((f32[64,64,32]{1,2,0:T(8,128)}), f32[64,64,32]{1,2,0:T(8,128)}) %all-reduce.8.cloned.1.call-update) | async-done | bytes 524304 | tf_op jit(solution)/shard_map/psum | solution.py:100
  110.6 35.9 %all-reduce.10.cloned.1.call-done = bf16[64,64,32]{1,2,0:T(8,128)(2,1)} async-done(((bf16[64,64,32]{1,2,0:T(8,128)(2,1)}), bf16[64,64,32]{1,2,0:T(8,128)(2,1)}) %all-reduce.10.cloned.1.call-update) | async-done | bytes 262160 | tf_op jit(solution)/shard_map/psum | solution.py:13
  146.5 3.2 convolution_bitcast_fusion.4
  149.8 21.6 %all-gather.2.cloned.1.call-done = bf16[64,256,32]{0,2,1:T(8,128)(2,1)} async-done(((bf16[64,64,32]{0,2,1:T(8,128)(2,1)}), bf16[64,256,32]{0,2,1:T(8,128)(2,1)}) %all-gather.2.cloned.1.call-update) | async-done | bytes 1048592 | tf_op jit(solution)/shard_map/all_gather | solution.py:58
  173.1 3.6 fusion.47
  184.4 2.7 copy.106
  192.6 2.7 copy.109
  200.4 2.7 copy.112
  209.0 2.7 copy.125
  211.7 2.7 copy.124
  214.4 2.7 copy.123
  217.1 4.1 %pad_maximum_fusion.1 = f32[64,64,32]{1,2,0:T(8,128)} fusion(f32[64,16,32]{1,2,0:T(8,128)} %copy.125, f32[64,16,32]{1,2,0:T(8,128)} %copy.124, f32[64,16,32]{1,2,0:T(8,128)} %copy.123, f32[64,16,32]{1,2,0:T(8,128)} %copy.122), kind=kLoop, calls=%fused_computation.68 | loop fusion | flops 393216 | bytes 1048576 | tf_op jit(solution)/shard_map/concatenate | solution.py:97
  222.5 2.7 copy.103
  227.3 2.9 fusion.42
  230.1 43.0 %all-reduce.6.cloned.1.call-done = f32[64,64,32]{1,2,0:T(8,128)} async-done(((f32[64,64,32]{1,2,0:T(8,128)}), f32[64,64,32]{1,2,0:T(8,128)}) %all-reduce.6.cloned.1.call-update) | async-done | bytes 524304 | tf_op jit(solution)/shard_map/psum | solution.py:98
  273.2 3.2 convolution_bitcast_fusion.5
  276.5 4.3 %fusion.43 = bf16[16,64,128]{2,1,0:T(8,128)(2,1)} fusion(bf16[16,64,1024]{1,2,0:T(8,128)(2,1)} %bitcast.150, bf16[1024,128]{1,0:T(8,128)(2,1)S(1)} %copy-done, f32[16,64]{1,0:T(8,128)S(1)} %copy-done.30), kind=kOutput, calls=%fused_computation.56 | convolution fusion | flops 268697600 | bytes 2625536 | tf_op jit(solution)/shard_map/ijk,kz->ijz/dot_general | solution.py:76
  283.9 3.6 fusion.95
  287.5 3.5 fusion.8
  291.0 16.1 %all-reduce.12.cloned.1.call-done = (f32[256,32]{0,1:T(8,128)}, f32[256,32]{0,1:T(8,128)}) async-done(((f32[256,32]{0,1:T(8,128)}, f32[256,32]{0,1:T(8,128)}), (f32[256,32]{0,1:T(8,128)}, f32[256,32]{0,1:T(8,128)})) %all-reduce.12.cloned.1.call-update) | async-done | bytes 65552 | tf_op jit(solution)/shard_map/psum | solution.py:112
  309.9 56.8 %reduce-scatter.2.cloned.1.call-done = f32[64,128]{1,0:T(8,128)} async-done(((f32[1024,128]{1,0:T(8,128)}), f32[64,128]{1,0:T(8,128)}) %reduce-scatter.2.cloned.1.call-update) | async-done | bytes 32784 | tf_op jit(solution)/shard_map/reduce_scatter | solution.py:113
  (137 shorter events, 59.1 us)
Async XLA Ops:
  7.2 15.2 %copy-start = (bf16[1024,128]{1,0:T(8,128)(2,1)S(1)}, bf16[1024,128]{1,0:T(8,128)(2,1)}, u32[]{:S(2)}) copy-start(bf16[1024,128]{1,0:T(8,128)(2,1)} %param.12) | copy-start | bytes 786436
  7.2 6.1 %copy-start.1 = (bf16[64,64,256]{2,1,0:T(8,128)(2,1)S(1)}, bf16[64,64,256]{2,1,0:T(8,128)(2,1)}, u32[]{:S(2)}) copy-start(bf16[64,64,256]{2,1,0:T(8,128)(2,1)} %param.7) | copy-start | bytes 6291460
  7.2 5.0 %copy-start.37 = (s32[256]{0:T(256)S(1)}, s32[256]{0:T(256)}, u32[]{:S(2)}) copy-start(s32[256]{0:T(256)} %param.9) | copy-start | bytes 3076
  7.2 5.0 %copy-start.26 = (s32[64,256]{1,0:T(8,128)S(1)}, s32[64,256]{1,0:T(8,128)}, u32[]{:S(2)}) copy-start(s32[64,256]{1,0:T(8,128)} %param.8) | copy-start | bytes 196612
  7.2 6.0 %copy-start.27 = (bf16[256,32]{0,1:T(8,128)(2,1)S(1)}, bf16[256,32]{0,1:T(8,128)(2,1)}, u32[]{:S(2)}) copy-start(bf16[256,32]{0,1:T(8,128)(2,1)} %param.10) | copy-start | bytes 49156
  7.2 97.6 %all-reduce.8.cloned.1.call-start = ((), (), s32[]{:S(2)}) async-start(), calls=%async_computation.3 | async-start | bytes 2097152 | tf_op jit(solution)/shard_map/psum | solution.py:100
  22.4 38.8 %copy-start.13 = (bf16[64,16,32]{0,2,1:T(8,128)(2,1)}, bf16[64,16,32]{0,2,1:T(8,128)(2,1)S(1)}, u32[]{:S(2)}) copy-start(bf16[64,16,32]{0,2,1:T(8,128)(2,1)S(1)} %copy.105) | copy-start | bytes 196612
  22.4 7.8 %copy-start.31 = (f32[16,64]{1,0:T(8,128)S(1)}, f32[16,64]{1,0:T(8,128)}, u32[]{:S(2)}) copy-start(f32[16,64]{1,0:T(8,128)} %get-tuple-element.14) | copy-start | bytes 12292
  30.3 8.0 %copy-start.33 = (f32[16,64]{1,0:T(8,128)S(1)}, f32[16,64]{1,0:T(8,128)}, u32[]{:S(2)}) copy-start(f32[16,64]{1,0:T(8,128)} %get-tuple-element.15) | copy-start | bytes 12292
  38.2 7.9 %copy-start.35 = (f32[16,64]{1,0:T(8,128)S(1)}, f32[16,64]{1,0:T(8,128)}, u32[]{:S(2)}) copy-start(f32[16,64]{1,0:T(8,128)} %get-tuple-element.16) | copy-start | bytes 12292
  54.4 3.8 %copy-start.2 = (bf16[16,64,1024]{1,2,0:T(8,128)(2,1)S(1)}, bf16[16,64,1024]{1,2,0:T(8,128)(2,1)}, u32[]{:S(2)}) copy-start(bf16[16,64,1024]{1,2,0:T(8,128)(2,1)} %copy.120) | copy-start | bytes 6291460
  54.4 3.8 %copy-start.9 = (bf16[64,16,32]{0,2,1:T(8,128)(2,1)S(1)}, bf16[64,16,32]{0,2,1:T(8,128)(2,1)}, u32[]{:S(2)}) copy-start(bf16[64,16,32]{0,2,1:T(8,128)(2,1)} %copy.111) | copy-start | bytes 196612
  54.4 5.3 %copy-start.4 = (bf16[16,64,1024]{1,2,0:T(8,128)(2,1)S(1)}, bf16[16,64,1024]{1,2,0:T(8,128)(2,1)}, u32[]{:S(2)}) copy-start(bf16[16,64,1024]{1,2,0:T(8,128)(2,1)} %copy.118) | copy-start | bytes 6291460
  54.4 5.3 %copy-start.11 = (bf16[64,16,32]{0,2,1:T(8,128)(2,1)S(1)}, bf16[64,16,32]{0,2,1:T(8,128)(2,1)}, u32[]{:S(2)}) copy-start(bf16[64,16,32]{0,2,1:T(8,128)(2,1)} %copy.108) | copy-start | bytes 196612
  62.6 42.2 %copy-start.20 = (f32[64,64]{1,0:T(8,128)S(1)}, f32[64,64]{1,0:T(8,128)}, u32[]{:S(2)}) copy-start(f32[64,64]{1,0:T(8,128)} %copy-done.19) | copy-start | bytes 49156
  62.6 44.4 %copy-start.17 = (f32[64,64]{1,0:T(8,128)S(1)}, f32[64,64]{1,0:T(8,128)}, u32[]{:S(2)}) copy-start(f32[64,64]{1,0:T(8,128)} %copy-done.16) | copy-start | bytes 49156
  62.6 44.4 %copy-start.24 = (f32[64,64]{1,0:T(8,128)S(1)}, f32[64,64]{1,0:T(8,128)}, u32[]{:S(2)}) copy-start(f32[64,64]{1,0:T(8,128)} %copy-done.23) | copy-start | bytes 49156
  62.6 44.4 %copy-start.28 = (bf16[256,32]{0,1:T(8,128)(2,1)S(1)}, bf16[256,32]{0,1:T(8,128)(2,1)}, u32[]{:S(2)}) copy-start(bf16[256,32]{0,1:T(8,128)(2,1)} %param.11) | copy-start | bytes 49156
  65.9 80.7 %all-reduce.10.cloned.1.call-start = ((), (), s32[]{:S(2)}) async-start(), calls=%async_computation.4 | async-start | bytes 1048576 | tf_op jit(solution)/shard_map/psum | solution.py:13
  107.0 64.4 %all-gather.2.cloned.1.call-start = ((), (), s32[]{:S(2)}) async-start(), calls=%async_computation.1 | async-start | bytes 2621440 | tf_op jit(solution)/shard_map/all_gather | solution.py:58
  110.5 162.6 %all-reduce.6.cloned.1.call-start = ((), (), s32[]{:S(2)}) async-start(), calls=%async_computation.2 | async-start | bytes 2097152 | tf_op jit(solution)/shard_map/psum | solution.py:98
  173.1 3.6 copy-start.3
  221.2 85.9 %all-reduce.12.cloned.1.call-start = ((), (), s32[]{:S(2)}) async-start(), calls=%async_computation.6 | async-start | bytes 131072 | tf_op jit(solution)/shard_map/psum | solution.py:112
  222.5 4.7 %copy-start.30 = (f32[16,64]{1,0:T(8,128)S(1)}, f32[16,64]{1,0:T(8,128)}, u32[]{:S(2)}) copy-start(f32[16,64]{1,0:T(8,128)} %get-tuple-element.13) | copy-start | bytes 12292
  222.5 4.7 %copy-start.39 = (f32[1024,128]{1,0:T(8,128)S(1)}, f32[1024,128]{1,0:T(8,128)}, u32[]{:S(2)}) copy-start(f32[1024,128]{1,0:T(8,128)} %convolution_bitcast_fusion.2) | copy-start | bytes 1572868
  222.5 4.7 %copy-start.40 = (f32[1024,128]{1,0:T(8,128)S(1)}, f32[1024,128]{1,0:T(8,128)}, u32[]{:S(2)}) copy-start(f32[1024,128]{1,0:T(8,128)} %convolution_bitcast_fusion.1) | copy-start | bytes 1572868
  222.5 4.7 %copy-start.41 = (f32[1024,128]{1,0:T(8,128)S(1)}, f32[1024,128]{1,0:T(8,128)}, u32[]{:S(2)}) copy-start(f32[1024,128]{1,0:T(8,128)} %convolution_bitcast_fusion) | copy-start | bytes 1572868
  227.2 45.9 %copy-start.18 = (f32[64,64]{1,0:T(8,128)S(1)}, f32[64,64]{1,0:T(8,128)}, u32[]{:S(2)}) copy-start(f32[64,64]{1,0:T(8,128)} %copy-done.16) | copy-start | bytes 49156
  227.3 45.9 %copy-start.21 = (f32[64,64]{1,0:T(8,128)S(1)}, f32[64,64]{1,0:T(8,128)}, u32[]{:S(2)}) copy-start(f32[64,64]{1,0:T(8,128)} %copy-done.19) | copy-start | bytes 49156
  227.3 45.9 %copy-start.25 = (f32[64,64]{1,0:T(8,128)S(1)}, f32[64,64]{1,0:T(8,128)}, u32[]{:S(2)}) copy-start(f32[64,64]{1,0:T(8,128)} %copy-done.23) | copy-start | bytes 49156
  276.4 6.7 %copy-start.15 = (f32[64,64,32]{1,2,0:T(8,128)S(1)}, f32[64,64,32]{1,2,0:T(8,128)}, u32[]{:S(2)}) copy-start(f32[64,64,32]{1,2,0:T(8,128)} %all-reduce.6.cloned.1.call-done) | copy-start | bytes 1572868
  276.4 90.3 %reduce-scatter.2.cloned.1.call-start = ((), (), s32[]{:S(2)}) async-start(), calls=%async_computation.5 | async-start | bytes 557056 | tf_op jit(solution)/shard_map/reduce_scatter | solution.py:113
  (16 other events, 37.3 us)
Sparse Core Ops, SparseCore 0:
  66.0 38.7 all-reduce.7
  107.8 38.6 all-reduce.9
  148.8 22.5 all-gather.1
  221.3 51.8 all-reduce.5
  276.5 30.5 all-reduce.11
  310.9 55.7 reduce-scatter.1
where the time goes:
time: 383 us; the launch traced here: 375 us
  waiting for transfers between devices  212 us (55%)
  matrix products  68.7 us (18%)
  local copies, waits for them, and re-layouts  54.3 us (14%)
  other arithmetic  24.4 us (6%)
  between operations  14.9 us (4%)
    reduce_scatter x1, waiting for transfers between devices, body(): lax.psum_scatter(output_gradient, ('row', 'col'), scatter_dimension=0, ti...  56.8 us
    psum x1, waiting for transfers between devices, body(): left_total = lax.psum(left_part, 'col')  43 us
    psum x1, waiting for transfers between devices, body(): right_full = lax.psum(right_acc, 'row')  38.9 us
    psum x1, waiting for transfers between devices, broadcast(): return lax.psum(jnp.where(mine, value, jnp.zeros_like(value)), axis)  35.9 us
    all_gather x1, waiting for transfers between devices, body(): every_right = lax.all_gather(right_own, 'row', axis=1, tiled=True)  21.6 us
    convert_element_type x4, local copies, waits for them, and re-layouts, body(): grad_outer = jnp.einsum('ijz,kz->ijk', scaled, output_weight, preferred_e...  19.7 us
    psum x1, waiting for transfers between devices, body(): first_factor_accrued, right_sum = lax.psum((left_wgrad, right_wgrad), 'row')  16.1 us
    dot_general x4, matrix products, body(): jnp.einsum('ijz,kz->ijk', scaled, output_weight, preferred_element_type=j...  12.2 us
  transfers between devices with their start and end apart: 6, of which 6 were waited for; matrix products, arithmetic and copies ran while one was open for 8% of the time, Pallas kernels for 0%

commit v1 on v0

v1 whole, which is shorter than its diff:
```python
import functools

import jax
import jax.numpy as jnp
from jax import lax
from jax.experimental import pallas as pl
from jax.experimental.pallas import tpu as pltpu
from jax.sharding import PartitionSpec as P

norm_eps = 1e-05
MESH = pl.DeviceIdType.MESH
NT = (((1,), (1,)), ((), ()))
TN = (((0,), (0,)), ((), ()))
VMEM = pl.BlockSpec(memory_space=pltpu.VMEM)
f32 = jnp.float32
bf16 = jnp.bfloat16


def layer_normalize(values):
    floats = values.astype(jnp.float32)
    average = jnp.mean(floats, -1, keepdims=True)
    centred = floats - average
    variance = jnp.mean(centred * centred, -1, keepdims=True)
    inverse_deviation = lax.rsqrt(variance + norm_eps)
    return (centred * inverse_deviation, inverse_deviation)


def spread_kernel(row_devs, ratio, own_ref, out_ref, send_sem, recv_sem):
    r = lax.axis_index("row")
    c = lax.axis_index("col")
    barrier = pltpu.get_barrier_semaphore()
    for d in range(1, row_devs):
        pl.semaphore_signal(
            barrier, inc=1, device_id={"row": lax.rem(r + d, row_devs)}, device_id_type=MESH
        )
    pl.semaphore_wait(barrier, row_devs - 1)

    def copy(k, d):
        return pltpu.make_async_remote_copy(
            src_ref=own_ref,
            dst_ref=out_ref.at[k],
            send_sem=send_sem.at[d],
            recv_sem=recv_sem.at[k],
            device_id={"row": lax.rem(r + d, row_devs)},
            device_id_type=MESH,
        )

    for k in range(ratio):

        @pl.when(c * ratio + k == r)
        def _():
            for d in range(1, row_devs):
                copy(k, d).start()
            out_ref[k] = own_ref[...]

    for k in range(ratio):

        @pl.when(c * ratio + k != r)
        def _():
            copy(k, 1).wait_recv()

        @pl.when(c * ratio + k == r)
        def _():
            for d in range(1, row_devs):
                copy(k, d).wait_send()


def spread_right(own, row_devs, ratio):
    return pl.pallas_call(
        functools.partial(spread_kernel, row_devs, ratio),
        out_shape=jax.ShapeDtypeStruct((ratio,) + own.shape, own.dtype),
        in_specs=[VMEM],
        out_specs=VMEM,
        scratch_shapes=[
            pltpu.SemaphoreType.DMA((row_devs,)),
            pltpu.SemaphoreType.DMA((ratio,)),
        ],
        compiler_params=pltpu.CompilerParams(collective_id=0, has_side_effects=True),
        name="spread_right",
    )(own)


def pair_kernel(
    ib,
    width,
    per,
    left_ref,
    right_ref,
    div_ref,
    cot_ref,
    wst_ref,
    wst2_ref,
    live_left_ref,
    live_right_ref,
    pair_ref,
    gleft_ref,
    gright_ref,
    gw_ref,
    x_ref,
    s_ref,
    gp_ref,
    gr_acc,
    gw_acc,
):
    step = pl.program_id(0)
    cols = cot_ref.shape[1]
    z = cot_ref.shape[2]
    tile = per * cols
    groups = width // per

    @pl.when(step == 0)
    def _():
        s_ref[...] = jnp.zeros_like(s_ref)
        gr_acc[...] = jnp.zeros_like(gr_acc)
        gw_acc[...] = jnp.zeros_like(gw_acc)

    left = left_ref[...]
    for g in range(groups):
        part = lax.dot_general(
            left, right_ref[:, g * tile : (g + 1) * tile], TN, preferred_element_type=f32
        ).astype(bf16)
        for i in range(ib):
            x_ref[g * width : (g + 1) * width, i * tile : (i + 1) * tile] = part[
                i * width : (i + 1) * width
            ]
    inverse = 1.0 / div_ref[0]
    for i in range(ib):
        scaled = (cot_ref[i].astype(f32) * inverse[:, i : i + 1]).astype(bf16)
        for p in range(per):
            s_ref[i * tile + p * cols : i * tile + (p + 1) * cols, p * z : (p + 1) * z] = scaled

    lanes = lax.broadcasted_iota(jnp.int32, (z, tile), 1)
    for i in range(ib):
        sl = slice(i * tile, (i + 1) * tile)
        y = jnp.dot(wst_ref[...], x_ref[:, sl], preferred_element_type=f32)
        picked = y[:z]
        for p in range(1, per):
            picked = jnp.where(lanes < p * cols, picked, y[p * z : (p + 1) * z])
        turned = picked.T
        total = turned[:cols]
        for p in range(1, per):
            total = total + turned[p * cols : (p + 1) * cols]
        pair_ref[i] = (total * inverse[:, i : i + 1]).astype(bf16)

    gw_acc[...] += jnp.dot(x_ref[...], s_ref[...], preferred_element_type=f32)

    for g in range(groups):
        rows = slice(g * width, (g + 1) * width)
        go = lax.dot_general(wst2_ref[rows], s_ref[...], NT, preferred_element_type=f32).astype(bf16)
        for i in range(ib):
            gp_ref[i * width : (i + 1) * width, g * tile : (g + 1) * tile] = go[
                :, i * tile : (i + 1) * tile
            ]
    gl = lax.dot_general(right_ref[...], gp_ref[...], NT, preferred_element_type=f32)
    gleft_ref[...] = (gl * live_left_ref[...].astype(f32)).astype(bf16)
    gr_acc[...] += jnp.dot(left, gp_ref[...], preferred_element_type=f32)

    @pl.when(step == pl.num_programs(0) - 1)
    def _():
        gright_ref[...] = (gr_acc[...] * live_right_ref[...].astype(f32)).astype(bf16)
        gw_ref[...] = gw_acc[...].astype(bf16)


def pair_block(left, right, divisor, cotangent, weight, live_left, live_right, width):
    rows, cols, z = cotangent.shape
    seqs = left.shape[0]
    ib = 8
    steps = rows // ib
    per = max(1, 128 // cols)
    tile = per * cols
    groups = width // per
    wst2 = weight.reshape(width, groups, per, z).transpose(1, 0, 2, 3)
    wst2 = wst2.reshape(groups * width, per * z)
    div = divisor.reshape(steps, ib, cols).transpose(0, 2, 1)
    whole = lambda shape: pl.BlockSpec(shape, lambda i: (0,) * len(shape))
    return pl.pallas_call(
        functools.partial(pair_kernel, ib, width, per),
        grid=(steps,),
        out_shape=(
            jax.ShapeDtypeStruct((rows, cols, z), bf16),
            jax.ShapeDtypeStruct((seqs, rows * width), bf16),
            jax.ShapeDtypeStruct((seqs, cols * width), bf16),
            jax.ShapeDtypeStruct((groups * width, per * z), bf16),
        ),
        in_specs=[
            pl.BlockSpec((seqs, ib * width), lambda i: (0, i)),
            whole((seqs, cols * width)),
            pl.BlockSpec((1, cols, ib), lambda i: (i, 0, 0)),
            pl.BlockSpec((ib, cols, z), lambda i: (i, 0, 0)),
            whole((per * z, groups * width)),
            whole((groups * width, per * z)),
            pl.BlockSpec((seqs, ib * width), lambda i: (0, i)),
            whole((seqs, cols * width)),
        ],
        out_specs=(
            pl.BlockSpec((ib, cols, z), lambda i: (i, 0, 0)),
            pl.BlockSpec((seqs, ib * width), lambda i: (0, i)),
            whole((seqs, cols * width)),
            whole((groups * width, per * z)),
        ),
        scratch_shapes=[
            pltpu.VMEM((groups * width, ib * tile), bf16),
            pltpu.VMEM((ib * tile, per * z), bf16),
            pltpu.VMEM((ib * width, groups * tile), bf16),
            pltpu.VMEM((seqs, cols * width), f32),
            pltpu.VMEM((groups * width, per * z), f32),
        ],
        compiler_params=pltpu.CompilerParams(vmem_limit_bytes=48 * 1024 * 1024),
        name="pair_block",
    )(left, right, div, cotangent, wst2.T, wst2, live_left, live_right)


def sums_kernel(
    row_devs,
    col_devs,
    ratio,
    scale,
    gl_ref,
    gr_ref,
    gw_ref,
    out_l,
    out_r,
    out_w,
    buf_l,
    buf_r,
    buf_w,
    done_l,
    done_r,
    l_send,
    l_recv,
    r_send,
    r_recv,
    w_send,
    w_recv,
    l2_send,
    l2_recv,
    r2_send,
    r2_recv,
):
    r = lax.axis_index("row")
    c = lax.axis_index("col")
    count = row_devs * col_devs
    me = r * col_devs + c

    def place(d):
        peer = lax.rem(me + d, count)
        return peer, {"row": peer // col_devs, "col": lax.rem(peer, col_devs)}

    barrier = pltpu.get_barrier_semaphore()
    for d in range(1, count):
        pl.semaphore_signal(barrier, inc=1, device_id=place(d)[1], device_id_type=MESH)
    pl.semaphore_wait(barrier, count - 1)

    def remote(src, dst, send, recv, where):
        return pltpu.make_async_remote_copy(
            src_ref=src,
            dst_ref=dst,
            send_sem=send,
            recv_sem=recv,
            device_id=where,
            device_id_type=MESH,
        )

    lefts, rights, outs = [], [], []
    for d in range(1, col_devs):
        peer = lax.rem(c + d, col_devs)
        lefts.append(
            remote(
                gl_ref.at[peer], buf_l.at[d - 1], l_send.at[d - 1], l_recv.at[d - 1], {"col": peer}
            )
        )
    for d in range(1, row_devs):
        peer = lax.rem(r + d, row_devs)
        rights.append(
            remote(
                gr_ref.at[peer], buf_r.at[d - 1], r_send.at[d - 1], r_recv.at[d - 1], {"row": peer}
            )
        )
    for d in range(1, count):
        peer, where = place(d)
        outs.append(
            remote(gw_ref.at[peer], buf_w.at[d - 1], w_send.at[d - 1], w_recv.at[d - 1], where)
        )
    for copy in rights + lefts + outs:
        copy.start()

    for copy in rights:
        copy.wait_recv()
    total = gr_ref[r].astype(f32)
    for d in range(1, row_devs):
        total = total + buf_r[d - 1].astype(f32)
    done_r[...] = total.astype(bf16)

    def right_copy(k, d):
        return remote(
            done_r.at[k],
            out_r.at[r],
            r2_send.at[k * col_devs + d],
            r2_recv.at[r],
            {"row": c * ratio + k, "col": lax.rem(c + d, col_devs)},
        )

    for k in range(ratio):
        for d in range(1, col_devs):
            right_copy(k, d).start()

        @pl.when(c * ratio + k == r)
        def _():
            out_r[r] = done_r[k]

        @pl.when(c * ratio + k != r)
        def _():
            right_copy(k, 0).start()

    for copy in lefts:
        copy.wait_recv()
    total = gl_ref[c].astype(f32)
    for d in range(1, col_devs):
        total = total + buf_l[d - 1].astype(f32)
    done_l[...] = total.astype(bf16)
    left_copies = []
    for d in range(1, col_devs):
        left_copies.append(
            remote(
                done_l,
                out_l.at[c],
                l2_send.at[d - 1],
                l2_recv.at[d - 1],
                {"col": lax.rem(c + d, col_devs)},
            )
        )
    for copy in left_copies:
        copy.start()
    out_l[c] = done_l[...]

    for copy in outs:
        copy.wait_recv()
    total = gw_ref[me].astype(f32)
    for d in range(1, count):
        total = total + buf_w[d - 1].astype(f32)
    out_w[...] = total * scale

    for copy in left_copies:
        copy.wait_recv()
    for src in range(row_devs):
        own = jnp.logical_and(r == src, c == r // ratio)

        @pl.when(jnp.logical_not(own))
        def _():
            remote(
                done_r.at[0], out_r.at[src], r2_send.at[0], r2_recv.at[src], {"col": c}
            ).wait_recv()

    for copy in rights + lefts + outs + left_copies:
        copy.wait_send()
    for k in range(ratio):
        for d in range(1, col_devs):
            right_copy(k, d).wait_send()

        @pl.when(c * ratio + k != r)
        def _():
            right_copy(k, 0).wait_send()


def device_sums(gl, gr, gw, row_devs, col_devs, ratio, scale):
    count = row_devs * col_devs
    dma = pltpu.SemaphoreType.DMA
    return pl.pallas_call(
        functools.partial(sums_kernel, row_devs, col_devs, ratio, scale),
        out_shape=(
            jax.ShapeDtypeStruct(gl.shape, bf16),
            jax.ShapeDtypeStruct((row_devs,) + gr.shape[2:], bf16),
            jax.ShapeDtypeStruct(gw.shape[1:], f32),
        ),
        in_specs=[VMEM] * 3,
        out_specs=(VMEM,) * 3,
        scratch_shapes=[
            pltpu.VMEM((col_devs - 1,) + gl.shape[1:], bf16),
            pltpu.VMEM((row_devs - 1,) + gr.shape[1:], bf16),
            pltpu.VMEM((count - 1,) + gw.shape[1:], bf16),
            pltpu.VMEM(gl.shape[1:], bf16),
            pltpu.VMEM(gr.shape[1:], bf16),
            dma((col_devs - 1,)),
            dma((col_devs - 1,)),
            dma((row_devs - 1,)),
            dma((row_devs - 1,)),
            dma((count - 1,)),
            dma((count - 1,)),
            dma((col_devs - 1,)),
            dma((col_devs - 1,)),
            dma((ratio * col_devs,)),
            dma((row_devs,)),
        ],
        compiler_params=pltpu.CompilerParams(
            collective_id=1, has_side_effects=True, vmem_limit_bytes=32 * 1024 * 1024
        ),
        name="device_sums",
    )(gl, gr, gw)


def weights_kernel(row_devs, scale, own_ref, out_ref, buf, send_sem, recv_sem):
    r = lax.axis_index("row")
    barrier = pltpu.get_barrier_semaphore()
    for d in range(1, row_devs):
        pl.semaphore_signal(
            barrier, inc=1, device_id={"row": lax.rem(r + d, row_devs)}, device_id_type=MESH
        )
    pl.semaphore_wait(barrier, row_devs - 1)
    copies = []
    for d in range(1, row_devs):
        copies.append(
            pltpu.make_async_remote_copy(
                src_ref=own_ref,
                dst_ref=buf.at[r],
                send_sem=send_sem.at[d - 1],
                recv_sem=recv_sem.at[d - 1],
                device_id={"row": lax.rem(r + d, row_devs)},
                device_id_type=MESH,
            )
        )
    for copy in copies:
        copy.start()
    buf[r] = own_ref[...]
    for copy in copies:
        copy.wait_recv()
    total = buf[0]
    for src in range(1, row_devs):
        total = total + buf[src]
    out_ref[...] = total * scale
    for copy in copies:
        copy.wait_send()


def sum_weights(own, row_devs, scale):
    return pl.pallas_call(
        functools.partial(weights_kernel, row_devs, scale),
        out_shape=jax.ShapeDtypeStruct(own.shape, f32),
        in_specs=[VMEM],
        out_specs=VMEM,
        scratch_shapes=[
            pltpu.VMEM((row_devs,) + own.shape, f32),
            pltpu.SemaphoreType.DMA((row_devs - 1,)),
            pltpu.SemaphoreType.DMA((row_devs - 1,)),
        ],
        compiler_params=pltpu.CompilerParams(collective_id=2, has_side_effects=True),
        name="sum_weights",
    )(own)


def body(
    alignment_activations,
    sequence_presence_flags,
    residue_padding_mask,
    left_weight,
    right_weight,
    output_weight,
    cotangent,
):
    row_idx = lax.axis_index("row")
    col_idx = lax.axis_index("col")
    row_devs = lax.axis_size("row")
    col_devs = lax.axis_size("col")
    ratio = row_devs // col_devs
    seqs, residues, channels = alignment_activations.shape
    residue_total = sequence_presence_flags.shape[1]
    cols = residue_total // col_devs
    width = left_weight.shape[1]
    z = output_weight.shape[1]
    count = row_devs * col_devs

    active_mask = (sequence_presence_flags * residue_padding_mask[None, :]).astype(f32)
    own_live = lax.dynamic_slice_in_dim(active_mask, row_idx * residues, residues, 1)
    live_cols = lax.dynamic_slice_in_dim(active_mask, col_idx * cols, cols, 1)
    unit, inverse_deviation = layer_normalize(alignment_activations)
    normed = unit.astype(bf16)
    right_own = jnp.einsum("snd,de->sen", normed, right_weight, preferred_element_type=f32)
    right_own = (right_own * own_live[:, None, :]).astype(bf16).reshape(seqs, width * residues)
    right = spread_right(right_own, row_devs, ratio)
    right = right.reshape(ratio, seqs, width, residues).transpose(1, 2, 0, 3)
    right = right.reshape(seqs, width * cols)
    left = jnp.einsum("snd,dc->snc", normed, left_weight, preferred_element_type=f32)
    left = (left * own_live[..., None]).astype(bf16).reshape(seqs, residues * width)
    divisor = jnp.maximum(jnp.dot(own_live.T, live_cols, precision=lax.Precision.HIGHEST), 1.0)
    live_left = jnp.repeat(own_live.astype(bf16), width, axis=1)
    live_right = jnp.tile(live_cols.astype(bf16), (1, width))

    pair, gl, gr, gw = pair_block(
        left, right, divisor, cotangent, output_weight, live_left, live_right, width
    )

    gl = gl.reshape(col_devs, 16, -1)
    gr = gr.reshape(row_devs, seqs // row_devs, width, ratio, residues)
    gr = gr.transpose(0, 3, 1, 2, 4).reshape(row_devs, ratio, 16, -1)
    per = gw.shape[1] // z
    gw = gw.reshape(width // per, width, per, z).transpose(1, 0, 2, 3)
    gw = gw.reshape(count, width * width // count, z)
    grad_left, grad_right, out_share = device_sums(
        gl, gr, gw, row_devs, col_devs, ratio, 1.0 / residue_total
    )
    grad_left = grad_left.reshape(seqs, residues, width)
    grad_right = grad_right.reshape(seqs, width, residues).transpose(0, 2, 1)
    grads = jnp.concatenate([grad_left, grad_right], -1)
    weights = jnp.concatenate([left_weight, right_weight], -1)
    wgrad = jnp.einsum("snd,snc->dc", normed, grads, preferred_element_type=f32)
    wgrad = sum_weights(wgrad, row_devs, 1.0 / residue_total)
    grad_normed = jnp.einsum("snc,dc->snd", grads, weights, preferred_element_type=f32)
    centered = (
        grad_normed
        - jnp.mean(grad_normed, -1, keepdims=True)
        - unit * jnp.mean(grad_normed * unit, -1, keepdims=True)
    )
    alignment_gradient = (inverse_deviation * centered).astype(bf16)
    return (pair, alignment_gradient, out_share, wgrad[:, :width], wgrad[:, width:])


def solution(mesh):
    return jax.shard_map(
        body,
        mesh=mesh,
        in_specs=(
            P("crop", "row", None),
            P("crop", None),
            P("crop"),
            P(),
            P(),
            P(),
            P(("crop", "row"), "col", None),
        ),
        out_specs=(
            P(("crop", "row"), "col", None),
            P("crop", "row", None),
            P(("crop", "row", "col"), None),
            P("crop", None),
            P("crop", None),
        ),
        check_vma=False,
    )
```

time: 383 us -> 120 us (0.31); the launches traced: 375 us -> 119 us
  waiting for transfers between devices: 212 us -> 0 us
  Pallas kernels: 0 us -> 80.7 us
  matrix products: 68.7 us -> 15.9 us
  local copies, waits for them, and re-layouts: 54.3 us -> 12.7 us
  other arithmetic: 24.4 us -> 8.4 us
  between operations: 14.9 us -> 0.96 us
    psum x4 -> x0, waiting for transfers between devices: 134 us -> none  [the longest x1 43 us: body(): left_total = lax.psum(left_part, 'col')]
    pallas_call x0 -> x4, Pallas kernels: none -> 80.7 us  [the longest x1 33 us: pair_block(): pl.pallas_call(functools.partial(pair_kernel, ib, width, per), grid=(step...]
    reduce_scatter x1 -> x0, waiting for transfers between devices: 56.8 us -> none  [body(): lax.psum_scatter(output_gradient, ('row', 'col'), scatter_dimension=0, ti...]
    dot_general x31 -> x5, matrix products: 68.7 us -> 15.9 us  [the longest x1 4.97 us: body(): wgrad = jnp.einsum('snd,snc->dc', normed, grads, preferred_element_type=f32)]
    convert_element_type x9 -> x3, local copies, waits for them, and re-layouts: 32.3 us -> 2.3 us  [the longest x1 2.13 us: body(): (left * own_live[..., None]).astype(bf16).reshape(seqs, residues * width)]
    all_gather x1 -> x0, waiting for transfers between devices: 21.6 us -> none  [body(): every_right = lax.all_gather(right_own, 'row', axis=1, tiled=True)]
    dot_general x4 -> x0, local copies, waits for them, and re-layouts: 9.9 us -> none  [body(): jnp.einsum('ijce,sje->sic', grad_outer, right_cols, preferred_element_typ...]
    slice x6 -> x1, local copies, waits for them, and re-layouts: 8.11 us -> 1.07 us  [body(): wgrad[:, width:]]
  transfers between devices with their start and end apart: 6 -> 0, of which waited for: 6 -> 0; matrix products, arithmetic and copies ran while one was open for 8% -> 0% of each run, Pallas kernels for 0% -> 0%
where the time goes in v1:
time: 120 us; the launch traced here: 119 us
  Pallas kernels  80.7 us (67%)
  matrix products  15.9 us (13%)
  local copies, waits for them, and re-layouts  12.7 us (11%)
  other arithmetic  8.4 us (7%)
    pallas_call x1, Pallas kernels, pair_block(): pl.pallas_call(functools.partial(pair_kernel, ib, width, per), grid=(step...  33 us
    pallas_call x1, Pallas kernels, device_sums(): pl.pallas_call(functools.partial(sums_kernel, row_devs, col_devs, ratio,...  27.5 us
    pallas_call x1, Pallas kernels, spread_right(): pl.pallas_call(functools.partial(spread_kernel, row_devs, ratio), out_sha...  11.3 us
    pallas_call x1, Pallas kernels, sum_weights(): pl.pallas_call(functools.partial(weights_kernel, row_devs, scale), out_sh...  8.9 us
    dot_general x1, matrix products, body(): wgrad = jnp.einsum('snd,snc->dc', normed, grads, preferred_element_type=f32)  4.97 us
    dot_general x1, matrix products, body(): jnp.einsum('snc,dc->snd', grads, weights, preferred_element_type=f32)  4.19 us
    dot_general x1, matrix products, body(): jnp.einsum('snd,dc->snc', normed, left_weight, preferred_element_type=f32)  3.58 us
    convert_element_type x1, other arithmetic, body(): alignment_gradient = (inverse_deviation * centered).astype(bf16)  3.5 us

profile of v1, /device:TPU:0, one launch (start us, length us, event | category | flops | bytes accessed | tf_op | source)
XLA Modules:
  0.0 118.6 jit_solution(4182529638230381922)
XLA Ops:
  0.7 2.3 %convert_reduce_fusion = f32[64,64]{1,0:T(8,128)S(1)} fusion(bf16[64,64,256]{2,1,0:T(8,128)(2,1)} %param.7), kind=kLoop, calls=%fused_computation.1 | loop fusion | flops 2093056 | bytes 2113536 | tf_op jit(solution)/shard_map/reduce_sum | solution.py:21
  3.0 2.5 %fusion.9 = f32[64,64]{1,0:T(8,128)S(1)} fusion(bf16[64,64,256]{2,1,0:T(8,128)(2,1)} %param.7, f32[64,64]{1,0:T(8,128)S(1)} %broadcast_multiply_fusion.2), kind=kLoop, calls=%fused_computation.11 | loop fusion | flops 4190208 | bytes 2129920 | tf_op jit(solution)/shard_map/reduce_sum | solution.py:23
  5.5 0.1 dynamic-slice_convert_fusion
  5.7 0.3 fusion.13
  6.0 0.1 copy.25
  6.1 0.1 copy.23
  6.2 0.2 copy.24
  6.5 0.1 copy.27.wst_ref
  6.7 0.2 copy.28.live_left_ref
  7.0 0.5 tile.10.live_right_ref
  7.5 2.9 %fusion.12 = bf16[64,32,64]{2,1,0:T(8,128)(2,1)S(1)} fusion(bf16[64,64,256]{2,1,0:T(8,128)(2,1)} %param.7, f32[64,64]{1,0:T(8,128)S(1)} %get-tuple-element.38, f32[64,64]{1,0:T(8,128)S(1)} %broadcast_multiply_fusion.2, f32[64,64]{1,0:T(8,128)S(1)} %get-tuple-element.32, bf16[256,32]{0,1:T(8,128)(2,1)S(1)} %copy-done.7), kind=kOutput, calls=%fused_computation.16 | convolution fusion | flops 71565312 | bytes 2424832 | tf_op jit(solution)/shard_map/snd,de->sen/dot_general | solution.py:476
  10.3 1.2 reshape.71.own_ref
  11.5 11.3 %spread_right.1 = bf16[1,64,2048]{2,1,0:T(8,128)(2,1)} custom-call(bf16[64,2048]{1,0:T(8,128)(2,1)} %reshape.71.own_ref), custom_call_target="tpu_custom_call" | custom-call | tf_op jit(solution)/shard_map/spread_right/pallas_call | solution.py:69
  22.9 3.6 %fusion.10 = bf16[64,64,32]{1,2,0:T(8,128)(2,1)} fusion(bf16[64,64,256]{2,1,0:T(8,128)(2,1)} %param.7, f32[64,64]{1,0:T(8,128)S(1)} %get-tuple-element.38, f32[64,64]{1,0:T(8,128)S(1)} %broadcast_multiply_fusion.2, f32[64,64]{1,0:T(8,128)S(1)} %get-tuple-element.32, bf16[256,32]{0,1:T(8,128)(2,1)S(1)} %copy-done.6), kind=kOutput, calls=%fused_computation.14 | convolution fusion | flops 71565312 | bytes 2424832 | tf_op jit(solution)/shard_map/snd,dc->snc/dot_general | solution.py:481
  26.5 2.1 %copy.22 = bf16[64,64,32]{0,2,1:T(8,128)(2,1)S(1)} copy(bf16[64,64,32]{1,2,0:T(8,128)(2,1)} %fusion.10) | data formatting | bytes 524288 | tf_op jit(solution)/shard_map/convert_element_type | solution.py:482
  28.6 0.2 copy.26.left_ref
  28.8 33.0 %pair_block.1 = (bf16[64,64,128]{2,1,0:T(8,128)(2,1)}, bf16[64,2048]{1,0:T(8,128)(2,1)S(1)}, bf16[64,2048]{1,0:T(8,128)(2,1)S(1)}, bf16[512,256]{1,0:T(8,128)(2,1)S(1)}) custom-call(bf16[64,2048]{1,0:T(8,128)(2,1)S(1)} %copy.26.left_ref, bf16[64,2048]{1,0:T(8,128)(2,1)S(1)} %bitcast.43, f32[8,64,8]{2,1,0:T(8,128)S(1)} %bitcast.42, ...), custom_call_target="tpu_custom_call" | custom-call | tf_op jit(solution)/shard_map/pair_block/pallas_call | solution.py:176
  61.8 0.7 copy-done.2
  62.5 1.0 reshape.77
  63.5 0.2 copy.29
  63.7 27.5 %device_sums.1 = (bf16[4,16,2048]{2,1,0:T(8,128)(2,1)S(1)}, bf16[4,16,2048]{2,1,0:T(8,128)(2,1)S(1)}, f32[64,128]{1,0:T(8,128)S(1)}) custom-call(bf16[4,16,2048]{2,1,0:T(8,128)(2,1)S(1)} %bitcast.44, bf16[4,1,16,2048]{3,2,1,0:T(8,128)(2,1)S(1)} %bitcast.45, bf16[16,64,128]{2,1,0:T(8,128)(2,1)S(1)} %bitcast.41), custom_call_target="tpu_custom_call" | custom-call | tf_op jit(solution)/shard_map/device_sums/pallas_call | solution.py:368
  91.2 0.5 reshape.80
  91.8 1.3 %copy.30 = bf16[64,32,64]{1,2,0:T(8,128)(2,1)} copy(bf16[64,32,64]{2,1,0:T(8,128)(2,1)S(1)} %reshape.80) | data formatting | bytes 524288 | tf_op jit(solution)/shard_map/reshape | solution.py:501
  93.1 0.8 reshape.79
  93.9 5.0 %convolution_bitcast_fusion.own_ref = f32[256,64]{1,0:T(8,128)} fusion(bf16[64,64,256]{2,1,0:T(8,128)(2,1)} %param.7, f32[64,64]{1,0:T(8,128)S(1)} %get-tuple-element.38, f32[64,64]{1,0:T(8,128)S(1)} %broadcast_multiply_fusion.2, bf16[64,64,32]{2,1,0:T(8,128)(2,1)} %bitcast.46, bf16[64,64,32]{2,1,0:T(8,128)(2,1)S(1)} %reshape.79), kind=kOutput, calls=%fused_computation.17 | convolution fusion | flops 139460608 | bytes 2719744 | tf_op jit(solution)/shard_map/snd,snc->dc/dot_general | solution.py:504
  98.9 8.9 %sum_weights.1 = f32[256,64]{1,0:T(8,128)} custom-call(f32[256,64]{1,0:T(8,128)} %convolution_bitcast_fusion.own_ref), custom_call_target="tpu_custom_call" | custom-call | tf_op jit(solution)/shard_map/sum_weights/pallas_call | solution.py:435
  107.8 1.1 fusion.29
  108.9 0.7 copy.35
  109.6 0.7 copy.34
  110.3 4.2 %fusion.27 = (f32[64,64]{1,0:T(8,128)S(1)}, f32[64,64]{1,0:T(8,128)S(1)}, f32[64,64,256]{2,1,0:T(8,128)S(1)}) fusion(f32[64,64]{1,0:T(8,128)S(1)} %get-tuple-element.38, f32[64,64]{1,0:T(8,128)S(1)} %broadcast_multiply_fusion.2, bf16[64,64,256]{2,1,0:T(8,128)(2,1)S(1)} %copy-done.3, bf16[256,32]{0,1:T(8,128)(2,1)S(1)} %copy-done.7, ...), kind=kOutput, calls=%fused_computation.40 | convolution fusion | flops 141615104 | bytes 6914048 | tf_op jit(solution)/shard_map/snc,dc->snd/dot_general | solution.py:506
  114.5 3.5 %fusion.8 = bf16[64,64,256]{2,1,0:T(8,128)(2,1)} fusion(bf16[64,64,256]{2,1,0:T(8,128)(2,1)S(1)} %copy-done.3, f32[64,64,256]{2,1,0:T(8,128)S(1)} %get-tuple-element.37, f32[64,64]{1,0:T(8,128)S(1)} %broadcast_multiply_fusion, f32[64,64]{1,0:T(8,128)S(1)} %broadcast_multiply_fusion.1, f32[64,64]{1,0:T(8,128)S(1)} %get-tuple-element.38, ...), kind=kLoop, calls=%fused_computation.10 | loop fusion | flops 8388608 | bytes 8454144 | tf_op jit(solution)/shard_map/convert_element_type | solution.py:512
  118.0 0.6 copy.46
  (25 shorter events, 0.3 us)
Async XLA Ops:
  0.6 5.6 %copy-start.4 = (bf16[1024,128]{1,0:T(8,128)(2,1)S(1)}, bf16[1024,128]{1,0:T(8,128)(2,1)}, u32[]{:S(2)}) copy-start(bf16[1024,128]{1,0:T(8,128)(2,1)} %param.12) | copy-start | bytes 786436
  0.6 4.8 %copy-start.8 = (s32[256]{0:T(256)S(1)}, s32[256]{0:T(256)}, u32[]{:S(2)}) copy-start(s32[256]{0:T(256)} %param.9) | copy-start | bytes 3076
  0.7 4.8 %copy-start.5 = (s32[64,256]{1,0:T(8,128)S(1)}, s32[64,256]{1,0:T(8,128)}, u32[]{:S(2)}) copy-start(s32[64,256]{1,0:T(8,128)} %param.8) | copy-start | bytes 196612
  0.7 6.8 %copy-start.7 = (bf16[256,32]{0,1:T(8,128)(2,1)S(1)}, bf16[256,32]{0,1:T(8,128)(2,1)}, u32[]{:S(2)}) copy-start(bf16[256,32]{0,1:T(8,128)(2,1)} %param.11) | copy-start | bytes 49156
  6.6 16.2 %copy-start.6 = (bf16[256,32]{0,1:T(8,128)(2,1)S(1)}, bf16[256,32]{0,1:T(8,128)(2,1)}, u32[]{:S(2)}) copy-start(bf16[256,32]{0,1:T(8,128)(2,1)} %param.10) | copy-start | bytes 49156
  10.3 18.5 %copy-start = (bf16[64,64,128]{2,1,0:T(8,128)(2,1)S(1)}, bf16[64,64,128]{2,1,0:T(8,128)(2,1)}, u32[]{:S(2)}) copy-start(bf16[64,64,128]{2,1,0:T(8,128)(2,1)} %cot_ref.1) | copy-start | bytes 3145732
  22.9 6.0 %copy-start.1 = (bf16[1,64,2048]{2,1,0:T(8,128)(2,1)S(1)}, bf16[1,64,2048]{2,1,0:T(8,128)(2,1)}, u32[]{:S(2)}) copy-start(bf16[1,64,2048]{2,1,0:T(8,128)(2,1)} %spread_right.1) | copy-start | bytes 786436
  61.8 0.7 copy-start.2
  93.9 16.4 %copy-start.3 = (bf16[64,64,256]{2,1,0:T(8,128)(2,1)S(1)}, bf16[64,64,256]{2,1,0:T(8,128)(2,1)}, u32[]{:S(2)}) copy-start(bf16[64,64,256]{2,1,0:T(8,128)(2,1)} %param.7) | copy-start | bytes 6291460

commit v2 on v1

v2 whole, which is shorter than its diff:
```python
import functools

import jax
import jax.numpy as jnp
from jax import lax
from jax.experimental import pallas as pl
from jax.experimental.pallas import tpu as pltpu
from jax.sharding import PartitionSpec as P

norm_eps = 1e-05
MESH = pl.DeviceIdType.MESH
NT = (((1,), (1,)), ((), ()))
TN = (((0,), (0,)), ((), ()))
VMEM = pl.BlockSpec(memory_space=pltpu.VMEM)
f32 = jnp.float32
bf16 = jnp.bfloat16


def layer_normalize(values):
    floats = values.astype(jnp.float32)
    average = jnp.mean(floats, -1, keepdims=True)
    centred = floats - average
    variance = jnp.mean(centred * centred, -1, keepdims=True)
    inverse_deviation = lax.rsqrt(variance + norm_eps)
    return (centred * inverse_deviation, inverse_deviation)


def pairs_kernel(
    row_devs,
    col_devs,
    ib,
    width,
    scale,
    own_ref,
    left_ref,
    div_ref,
    cot_ref,
    wst_ref,
    wst2_ref,
    live_left_ref,
    live_right_ref,
    pair_ref,
    out_l,
    out_r,
    out_w,
    got,
    right_ref,
    x_ref,
    s_ref,
    gp_ref,
    gw_acc,
    gl_ref,
    gr_ref,
    gw_ref,
    buf_l,
    buf_r,
    buf_w,
    done_l,
    done_r,
    a_send,
    a_recv,
    l_send,
    l_recv,
    r_send,
    r_recv,
    w_send,
    w_recv,
    l2_send,
    l2_recv,
    r2_send,
    r2_recv,
):
    r = lax.axis_index("row")
    c = lax.axis_index("col")
    ratio = row_devs // col_devs
    count = row_devs * col_devs
    me = r * col_devs + c
    rows, cols, z = cot_ref.shape
    seqs = left_ref.shape[0]
    per = wst_ref.shape[0] // z
    tile = per * cols
    groups = width // per
    steps = rows // ib
    residues = cols // ratio

    def place(d):
        peer = lax.rem(me + d, count)
        return peer, {"row": peer // col_devs, "col": lax.rem(peer, col_devs)}

    def remote(src, dst, send, recv, where):
        return pltpu.make_async_remote_copy(
            src_ref=src,
            dst_ref=dst,
            send_sem=send,
            recv_sem=recv,
            device_id=where,
            device_id_type=MESH,
        )

    barrier = pltpu.get_barrier_semaphore()
    for d in range(1, count):
        pl.semaphore_signal(barrier, inc=1, device_id=place(d)[1], device_id_type=MESH)
    pl.semaphore_wait(barrier, count - 1)

    def spread(k, d):
        where = {"row": lax.rem(r + d, row_devs)}
        return remote(own_ref, got.at[k], a_send.at[d], a_recv.at[k], where)

    for k in range(ratio):

        @pl.when(c * ratio + k == r)
        def _():
            for d in range(1, row_devs):
                spread(k, d).start()
            got[k] = own_ref[...]

    def grad_step(b, carry):
        inverse = 1.0 / div_ref[b]
        base = pl.multiple_of(b * (ib * tile), ib * tile)
        for i in range(ib):
            scaled = (cot_ref[b * ib + i].astype(f32) * inverse[:, i : i + 1]).astype(bf16)
            for p in range(per):
                at = pl.ds(base + i * tile + p * cols, cols)
                for q in range(per):
                    s_ref[at, q * z : (q + 1) * z] = scaled if p == q else jnp.zeros_like(scaled)
        block = s_ref[pl.ds(base, ib * tile)]
        first = pl.multiple_of(b * (ib * width), ib * width)
        for g in range(groups):
            part = slice(g * width, (g + 1) * width)
            go = lax.dot_general(wst2_ref[part], block, NT, preferred_element_type=f32)
            go = go.astype(bf16)
            for i in range(ib):
                gp_ref[pl.ds(first + i * width, width), g * tile : (g + 1) * tile] = go[
                    :, i * tile : (i + 1) * tile
                ]
        return carry

    lax.fori_loop(0, steps, grad_step, 0)

    for k in range(ratio):

        @pl.when(c * ratio + k != r)
        def _():
            spread(k, 1).wait_recv()

    if ratio == 1:
        right_ref[...] = got[0]
    else:
        for k in range(ratio):
            for e in range(width):
                at = e * cols + k * residues
                right_ref[:, at : at + residues] = got[k, :, e * residues : (e + 1) * residues]

    wide = 256
    slab = seqs // row_devs
    for n in range(0, cols * width, wide):
        gr = jnp.dot(left_ref[...], gp_ref[:, n : n + wide], preferred_element_type=f32)
        gr = (gr * live_right_ref[:, n : n + wide].astype(f32)).astype(bf16)
        for src in range(row_devs):
            piece = gr[src * slab : (src + 1) * slab]
            if ratio == 1:
                gr_ref[src, 0, :, n : n + wide] = piece
            else:
                for o in range(0, wide, residues):
                    e, k = (n + o) // cols, (n + o) % cols // residues
                    gr_ref[src, k, :, e * residues : (e + 1) * residues] = piece[:, o : o + residues]
    rights = []
    for d in range(1, row_devs):
        peer = lax.rem(r + d, row_devs)
        rights.append(
            remote(
                gr_ref.at[peer], buf_r.at[d - 1], r_send.at[d - 1], r_recv.at[d - 1], {"row": peer}
            )
        )
    for copy in rights:
        copy.start()

    slab_l = seqs // col_devs
    for n in range(0, rows * width, wide):
        gl = lax.dot_general(
            right_ref[...], gp_ref[n : n + wide], NT, preferred_element_type=f32
        )
        gl = (gl * live_left_ref[:, n : n + wide].astype(f32)).astype(bf16)
        for src in range(col_devs):
            gl_ref[src, :, n : n + wide] = gl[src * slab_l : (src + 1) * slab_l]
    lefts = []
    for d in range(1, col_devs):
        peer = lax.rem(c + d, col_devs)
        lefts.append(
            remote(
                gl_ref.at[peer], buf_l.at[d - 1], l_send.at[d - 1], l_recv.at[d - 1], {"col": peer}
            )
        )
    for copy in lefts:
        copy.start()

    gw_acc[...] = jnp.zeros_like(gw_acc)
    lanes = lax.broadcasted_iota(jnp.int32, (z, tile), 1)

    def pair_step(b, carry):
        left = left_ref[:, pl.ds(pl.multiple_of(b * (ib * width), ib * width), ib * width)]
        for g in range(groups):
            part = lax.dot_general(
                left, right_ref[:, g * tile : (g + 1) * tile], TN, preferred_element_type=f32
            ).astype(bf16)
            for i in range(ib):
                x_ref[g * width : (g + 1) * width, i * tile : (i + 1) * tile] = part[
                    i * width : (i + 1) * width
                ]
        inverse = 1.0 / div_ref[b]
        for i in range(ib):
            sl = slice(i * tile, (i + 1) * tile)
            y = jnp.dot(wst_ref[...], x_ref[:, sl], preferred_element_type=f32)
            picked = y[:z]
            for p in range(1, per):
                picked = jnp.where(lanes < p * cols, picked, y[p * z : (p + 1) * z])
            turned = picked.T
            total = turned[:cols]
            for p in range(1, per):
                total = total + turned[p * cols : (p + 1) * cols]
            pair_ref[b * ib + i] = (total * inverse[:, i : i + 1]).astype(bf16)
        block = s_ref[pl.ds(pl.multiple_of(b * (ib * tile), ib * tile), ib * tile)]
        share = jnp.dot(x_ref[...], block, preferred_element_type=f32)
        gw_acc[...] += share.reshape(groups, width, per * z)
        return carry

    lax.fori_loop(0, steps // 2, pair_step, 0)

    for copy in rights:
        copy.wait_recv()
    total = gr_ref[r].astype(f32)
    for d in range(1, row_devs):
        total = total + buf_r[d - 1].astype(f32)
    done_r[...] = total.astype(bf16)

    def right_copy(k, d):
        return remote(
            done_r.at[k],
            out_r.at[r],
            r2_send.at[k * col_devs + d],
            r2_recv.at[r],
            {"row": c * ratio + k, "col": lax.rem(c + d, col_devs)},
        )

    for k in range(ratio):
        for d in range(1, col_devs):
            right_copy(k, d).start()

        @pl.when(c * ratio + k == r)
        def _():
            out_r[r] = done_r[k]

        @pl.when(c * ratio + k != r)
        def _():
            right_copy(k, 0).start()

    for copy in lefts:
        copy.wait_recv()
    total = gl_ref[c].astype(f32)
    for d in range(1, col_devs):
        total = total + buf_l[d - 1].astype(f32)
    done_l[...] = total.astype(bf16)
    left_copies = []
    for d in range(1, col_devs):
        where = {"col": lax.rem(c + d, col_devs)}
        left_copies.append(
            remote(done_l, out_l.at[c], l2_send.at[d - 1], l2_recv.at[d - 1], where)
        )
    for copy in left_copies:
        copy.start()
    out_l[c] = done_l[...]

    lax.fori_loop(steps // 2, steps, pair_step, 0)

    chunk = out_w.shape[0]
    piece = min(groups, chunk)
    for ch in range(width):
        row = gw_acc[:, ch, :].astype(bf16)
        for p in range(per):
            for o in range(0, groups, piece):
                flat = (ch * per + p) * groups + o
                at = flat % chunk
                gw_ref[flat // chunk, at : at + piece] = row[o : o + piece, p * z : (p + 1) * z]
    outs = []
    for d in range(1, count):
        peer, where = place(d)
        outs.append(
            remote(gw_ref.at[peer], buf_w.at[d - 1], w_send.at[d - 1], w_recv.at[d - 1], where)
        )
    for copy in outs:
        copy.start()

    for copy in left_copies:
        copy.wait_recv()
    for src in range(row_devs):
        own = jnp.logical_and(r == src, c == r // ratio)

        @pl.when(jnp.logical_not(own))
        def _():
            where = {"col": lax.rem(c + 1, col_devs)}
            remote(
                done_r.at[0], out_r.at[src], r2_send.at[0], r2_recv.at[src], where
            ).wait_recv()

    for copy in outs:
        copy.wait_recv()
    total = gw_ref[me].astype(f32)
    for d in range(1, count):
        total = total + buf_w[d - 1].astype(f32)
    total = total * scale
    if per == 1:
        out_w[...] = total
    else:
        for o in range(0, chunk, groups):
            ch, p = o // groups // per, o // groups % per
            out_w[pl.ds(ch * width + p, groups, stride=per), :] = total[o : o + groups]

    for copy in rights + lefts + outs + left_copies:
        copy.wait_send()
    for k in range(ratio):

        @pl.when(c * ratio + k == r)
        def _():
            for d in range(1, row_devs):
                spread(k, d).wait_send()

        for d in range(1, col_devs):
            right_copy(k, d).wait_send()

        @pl.when(c * ratio + k != r)
        def _():
            right_copy(k, 0).wait_send()


def pairs(
    own, left, divisor, cotangent, weight, live_left, live_right, width, row_devs, col_devs, scale
):
    rows, cols, z = cotangent.shape
    seqs = left.shape[0]
    ib = 8
    steps = rows // ib
    per = max(1, 128 // cols)
    tile = per * cols
    groups = width // per
    ratio = row_devs // col_devs
    count = row_devs * col_devs
    residues = cols // ratio
    chunk = width * width // count
    wst2 = weight.reshape(width, groups, per, z).transpose(1, 0, 2, 3)
    wst2 = wst2.reshape(groups * width, per * z)
    div = divisor.reshape(steps, ib, cols).transpose(0, 2, 1)
    dma = pltpu.SemaphoreType.DMA
    vmem = pltpu.VMEM
    l_shape = (seqs // col_devs, rows * width)
    r_shape = (seqs // row_devs, residues * width)
    return pl.pallas_call(
        functools.partial(pairs_kernel, row_devs, col_devs, ib, width, scale),
        out_shape=(
            jax.ShapeDtypeStruct((rows, cols, z), bf16),
            jax.ShapeDtypeStruct((col_devs,) + l_shape, bf16),
            jax.ShapeDtypeStruct((row_devs,) + r_shape, bf16),
            jax.ShapeDtypeStruct((chunk, z), f32),
        ),
        in_specs=[VMEM] * 8,
        out_specs=(VMEM,) * 4,
        scratch_shapes=[
            vmem((ratio, seqs, residues * width), bf16),
            vmem((seqs, cols * width), bf16),
            vmem((groups * width, ib * tile), bf16),
            vmem((rows * tile, per * z), bf16),
            vmem((rows * width, groups * tile), bf16),
            vmem((groups, width, per * z), f32),
            vmem((col_devs,) + l_shape, bf16),
            vmem((row_devs, ratio) + r_shape, bf16),
            vmem((count, chunk, z), bf16),
            vmem((col_devs - 1,) + l_shape, bf16),
            vmem((row_devs - 1, ratio) + r_shape, bf16),
            vmem((count - 1, chunk, z), bf16),
            vmem(l_shape, bf16),
            vmem((ratio,) + r_shape, bf16),
            dma((row_devs,)),
            dma((ratio,)),
            dma((col_devs - 1,)),
            dma((col_devs - 1,)),
            dma((row_devs - 1,)),
            dma((row_devs - 1,)),
            dma((count - 1,)),
            dma((count - 1,)),
            dma((col_devs - 1,)),
            dma((col_devs - 1,)),
            dma((ratio * col_devs,)),
            dma((row_devs,)),
        ],
        compiler_params=pltpu.CompilerParams(
            collective_id=0, has_side_effects=True, vmem_limit_bytes=52 * 1024 * 1024
        ),
        name="pairs",
    )(own, left, div, cotangent, wst2.T, wst2, live_left, live_right)


def tail_kernel(
    row_devs,
    scale,
    x_ref,
    grads_ref,
    weights_ref,
    align_ref,
    left_ref,
    right_ref,
    buf,
    unit_ref,
    inv_ref,
    send_sem,
    recv_sem,
):
    r = lax.axis_index("row")
    rows = 512
    steps = x_ref.shape[0] // rows
    barrier = pltpu.get_barrier_semaphore()
    for d in range(1, row_devs):
        where = {"row": lax.rem(r + d, row_devs)}
        pl.semaphore_signal(barrier, inc=1, device_id=where, device_id_type=MESH)

    def weight_step(b, total):
        at = pl.ds(pl.multiple_of(b * rows, rows), rows)
        unit, inverse = layer_normalize(x_ref[at])
        unit_ref[at] = unit
        inv_ref[at] = inverse
        return total + lax.dot_general(
            grads_ref[at], unit.astype(bf16), TN, preferred_element_type=f32
        )

    total = lax.fori_loop(0, steps, weight_step, jnp.zeros(buf.shape[1:], f32))
    buf[r] = total
    pl.semaphore_wait(barrier, row_devs - 1)
    copies = []
    for d in range(1, row_devs):
        copies.append(
            pltpu.make_async_remote_copy(
                src_ref=buf.at[r],
                dst_ref=buf.at[r],
                send_sem=send_sem.at[d - 1],
                recv_sem=recv_sem.at[d - 1],
                device_id={"row": lax.rem(r + d, row_devs)},
                device_id_type=MESH,
            )
        )
    for copy in copies:
        copy.start()

    def input_step(b, carry):
        at = pl.ds(pl.multiple_of(b * rows, rows), rows)
        unit = unit_ref[at]
        grad = lax.dot_general(grads_ref[at], weights_ref[...], NT, preferred_element_type=f32)
        grad = (
            grad
            - jnp.mean(grad, -1, keepdims=True)
            - unit * jnp.mean(grad * unit, -1, keepdims=True)
        )
        align_ref[at] = (inv_ref[at] * grad).astype(bf16)
        return carry

    lax.fori_loop(0, steps, input_step, 0)
    for d in range(1, row_devs):
        src = lax.rem(r - d + row_devs, row_devs)
        pltpu.make_async_remote_copy(
            src_ref=buf.at[src],
            dst_ref=buf.at[src],
            send_sem=send_sem.at[d - 1],
            recv_sem=recv_sem.at[d - 1],
            device_id={"row": lax.rem(r + d, row_devs)},
            device_id_type=MESH,
        ).wait_recv()
    total = buf[0]
    for src in range(1, row_devs):
        total = total + buf[src]
    total = (total * scale).T
    width = left_ref.shape[1]
    left_ref[...] = total[:, :width]
    right_ref[...] = total[:, width:]
    for copy in copies:
        copy.wait_send()


def tail(x, grads, weights, row_devs, scale):
    rows, channels = x.shape
    both = grads.shape[1]
    width = both // 2
    return pl.pallas_call(
        functools.partial(tail_kernel, row_devs, scale),
        out_shape=(
            jax.ShapeDtypeStruct(x.shape, bf16),
            jax.ShapeDtypeStruct((channels, width), f32),
            jax.ShapeDtypeStruct((channels, width), f32),
        ),
        in_specs=[VMEM] * 3,
        out_specs=(VMEM,) * 3,
        scratch_shapes=[
            pltpu.VMEM((row_devs, both, channels), f32),
            pltpu.VMEM((rows, channels), f32),
            pltpu.VMEM((rows, 1), f32),
            pltpu.SemaphoreType.DMA((row_devs - 1,)),
            pltpu.SemaphoreType.DMA((row_devs - 1,)),
        ],
        compiler_params=pltpu.CompilerParams(
            collective_id=1, has_side_effects=True, vmem_limit_bytes=48 * 1024 * 1024
        ),
        name="tail",
    )(x, grads, weights)


def body(
    alignment_activations,
    sequence_presence_flags,
    residue_padding_mask,
    left_weight,
    right_weight,
    output_weight,
    cotangent,
):
    row_idx = lax.axis_index("row")
    col_idx = lax.axis_index("col")
    row_devs = lax.axis_size("row")
    col_devs = lax.axis_size("col")
    seqs, residues, channels = alignment_activations.shape
    residue_total = sequence_presence_flags.shape[1]
    cols = residue_total // col_devs
    width = left_weight.shape[1]

    active_mask = (sequence_presence_flags * residue_padding_mask[None, :]).astype(f32)
    own_live = lax.dynamic_slice_in_dim(active_mask, row_idx * residues, residues, 1)
    live_cols = lax.dynamic_slice_in_dim(active_mask, col_idx * cols, cols, 1)
    unit, _ = layer_normalize(alignment_activations)
    normed = unit.astype(bf16)
    right_own = jnp.einsum("snd,de->sen", normed, right_weight, preferred_element_type=f32)
    right_own = (right_own * own_live[:, None, :]).astype(bf16).reshape(seqs, width * residues)
    left = jnp.einsum("snd,dc->snc", normed, left_weight, preferred_element_type=f32)
    left = (left * own_live[..., None]).astype(bf16).reshape(seqs, residues * width)
    divisor = jnp.maximum(jnp.dot(own_live.T, live_cols, precision=lax.Precision.HIGHEST), 1.0)
    live_left = jnp.repeat(own_live.astype(bf16), width, axis=1)
    live_right = jnp.tile(live_cols.astype(bf16), (1, width))

    pair, grad_left, grad_right, out_share = pairs(
        right_own,
        left,
        divisor,
        cotangent,
        output_weight,
        live_left,
        live_right,
        width,
        row_devs,
        col_devs,
        1.0 / residue_total,
    )
    grad_left = grad_left.reshape(seqs, residues, width)
    grad_right = grad_right.reshape(seqs, width, residues).transpose(0, 2, 1)
    grads = jnp.concatenate([grad_left, grad_right], -1).reshape(seqs * residues, 2 * width)
    weights = jnp.concatenate([left_weight, right_weight], -1)
    flat = alignment_activations.reshape(seqs * residues, channels)
    align, left_wgrad, right_wgrad = tail(flat, grads, weights, row_devs, 1.0 / residue_total)
    align = align.reshape(seqs, residues, channels)
    return (pair, align, out_share, left_wgrad, right_wgrad)


def solution(mesh):
    return jax.shard_map(
        body,
        mesh=mesh,
        in_specs=(
            P("crop", "row", None),
            P("crop", None),
            P("crop"),
            P(),
            P(),
            P(),
            P(("crop", "row"), "col", None),
        ),
        out_specs=(
            P(("crop", "row"), "col", None),
            P("crop", "row", None),
            P(("crop", "row", "col"), None),
            P("crop", None),
            P("crop", None),
        ),
        check_vma=False,
    )
```

time: 120 us -> 99.3 us (0.83)
  Pallas kernels: 80.7 us -> 66.2 us
  matrix products: 15.9 us -> 5.68 us
  local copies, waits for them, and re-layouts: 12.7 us -> 19.7 us
  other arithmetic: 8.4 us -> 6.2 us
    pallas_call x4 -> x2, Pallas kernels: 80.7 us -> 66.2 us  [the longest x1 59.3 us: pairs(): pl.pallas_call(functools.partial(pairs_kernel, row_devs, col_devs, ib, wi...]
    dot_general x2 -> x0, matrix products: 9.16 us -> none  [the longest x1 4.97 us: body(): wgrad = jnp.einsum('snd,snc->dc', normed, grads, preferred_element_type=f32)]
    unnamed x22 -> x38, local copies, waits for them, and re-layouts: 2.78 us -> 7.32 us
    convert_element_type x1 -> x0, other arithmetic: 3.5 us -> none  [body(): alignment_gradient = (inverse_deviation * centered).astype(bf16)]
    reshape x5 -> x2, local copies, waits for them, and re-layouts: 2.36 us -> 0.36 us  [the longest x1 0.24 us: pairs(): wst2 = weight.reshape(width, groups, per, z).transpose(1, 0, 2, 3)]
    concatenate x0 -> x2, other arithmetic: none -> 1.9 us  [the longest x1 1.81 us: body(): jnp.concatenate([grad_left, grad_right], -1)]
    reduce_sum x1, other arithmetic: 2.53 us -> 1.31 us  [layer_normalize(): variance = jnp.mean(centred * centred, -1, keepdims=True)]
    dot_general x1, matrix products: 3.58 us -> 2.38 us  [body(): jnp.einsum('snd,dc->snc', normed, left_weight, preferred_element_type=f32)]
where the time goes in v2:
time: 99.3 us; the launch traced here: 98.7 us
  Pallas kernels  66.2 us (67%)
  local copies, waits for them, and re-layouts  19.7 us (20%)
  other arithmetic  6.2 us (6%)
  matrix products  5.68 us (6%)
    pallas_call x1, Pallas kernels, pairs(): pl.pallas_call(functools.partial(pairs_kernel, row_devs, col_devs, ib, wi...  59.3 us
    unnamed x38, local copies, waits for them, and re-layouts  7.32 us
    pallas_call x1, Pallas kernels, tail(): pl.pallas_call(functools.partial(tail_kernel, row_devs, scale), out_shape...  6.85 us
    dot_general x1, matrix products, body(): jnp.einsum('snd,de->sen', normed, right_weight, preferred_element_type=f32)  3.04 us
    reshape x2, local copies, waits for them, and re-layouts, body(): grad_right = grad_right.reshape(seqs, width, residues).transpose(0, 2, 1)  2.85 us
    dot_general x1, matrix products, body(): jnp.einsum('snd,dc->snc', normed, left_weight, preferred_element_type=f32)  2.38 us
    reduce_sum x1, other arithmetic, layer_normalize(): average = jnp.mean(floats, -1, keepdims=True)  2.35 us

profile of v2, /device:TPU:0, one launch (start us, length us, event | category | flops | bytes accessed | tf_op | source)
XLA Modules:
  0.0 98.7 jit_solution(7177605379102482257)
XLA Ops:
  0.7 2.3 %convert_reduce_fusion = f32[64,64]{1,0:T(8,128)S(1)} fusion(bf16[64,64,256]{2,1,0:T(8,128)(2,1)} %param.7), kind=kLoop, calls=%fused_computation.1 | loop fusion | flops 2093056 | bytes 2113536 | tf_op jit(solution)/shard_map/reduce_sum | solution.py:21
  3.1 1.3 %fusion.2 = f32[64,64]{1,0:T(8,128)S(1)} fusion(bf16[64,64,256]{2,1,0:T(8,128)(2,1)S(1)} %copy-done, f32[64,64]{1,0:T(8,128)S(1)} %broadcast_multiply_fusion), kind=kLoop, calls=%fused_computation.4 | loop fusion | flops 4190208 | bytes 2129920 | tf_op jit(solution)/shard_map/reduce_sum | solution.py:23
  4.5 0.6 fusion.29
  5.1 0.3 fusion.23
  5.4 0.7 copy.23
  6.1 0.1 copy.28
  6.2 0.1 copy.29
  6.5 0.1 copy.21
  6.6 0.2 copy.22
  6.9 0.1 copy.25.wst_ref
  7.1 0.8 broadcast_in_dim.2
  7.9 0.9 copy.26.live_left_ref
  8.8 1.2 %tile.10.live_right_ref = bf16[64,2048]{1,0:T(8,128)(2,1)} reshape(bf16[64,32,64]{2,1,0:T(8,128)(2,1)S(1)} %tile.4) | data formatting | bytes 524288 | tf_op jit(solution)/shard_map/tile | solution.py:541
  10.0 2.4 %fusion.14 = bf16[64,64,32]{1,2,0:T(8,128)(2,1)S(1)} fusion(bf16[64,64,256]{2,1,0:T(8,128)(2,1)S(1)} %copy-done, f32[64,64]{1,0:T(8,128)} %get-tuple-element.33, f32[64,64]{1,0:T(8,128)S(1)} %broadcast_multiply_fusion, f32[64,64]{1,0:T(8,128)S(1)} %copy-done.9, bf16[256,32]{0,1:T(8,128)(2,1)} %param.10), kind=kOutput, calls=%fused_computation.10 | convolution fusion | flops 71565312 | bytes 2424832 | tf_op jit(solution)/shard_map/snd,dc->snc/dot_general | solution.py:537
  12.4 1.8 %copy.20 = bf16[64,64,32]{0,2,1:T(8,128)(2,1)} copy(bf16[64,64,32]{1,2,0:T(8,128)(2,1)S(1)} %fusion.14) | data formatting | bytes 524288 | tf_op jit(solution)/shard_map/convert_element_type | solution.py:538
  14.2 1.2 %copy.24.left_ref = bf16[64,2048]{1,0:T(8,128)(2,1)S(1)} copy(bf16[64,2048]{0,1:T(8,128)(2,1)} %bitcast.37) | data formatting | bytes 524288 | tf_op jit(solution)/shard_map/reshape | solution.py:538
  15.5 3.0 %fusion.20 = bf16[64,32,64]{2,1,0:T(8,128)(2,1)} fusion(bf16[64,64,256]{2,1,0:T(8,128)(2,1)S(1)} %copy-done, f32[64,64]{1,0:T(8,128)} %get-tuple-element.33, f32[64,64]{1,0:T(8,128)S(1)} %broadcast_multiply_fusion, f32[64,64]{1,0:T(8,128)S(1)} %copy-done.9, bf16[256,32]{0,1:T(8,128)(2,1)S(1)} %copy-done.13), kind=kOutput, calls=%fused_computation.12 | convolution fusion | flops 71565312 | bytes 2424832 | tf_op jit(solution)/shard_map/snd,de->sen/dot_general | solution.py:535
  18.5 1.5 %reshape.61.own_ref = bf16[64,2048]{1,0:T(8,128)(2,1)S(1)} reshape(bf16[64,32,64]{2,1,0:T(8,128)(2,1)} %fusion.20) | data formatting | bytes 524288 | tf_op jit(solution)/shard_map/reshape | solution.py:536
  20.0 59.3 %pairs.1 = (bf16[64,64,128]{2,1,0:T(8,128)(2,1)}, bf16[4,16,2048]{2,1,0:T(8,128)(2,1)S(1)}, bf16[4,16,2048]{2,1,0:T(8,128)(2,1)S(1)}, f32[64,128]{1,0:T(8,128)S(1)}) custom-call(bf16[64,2048]{1,0:T(8,128)(2,1)S(1)} %reshape.61.own_ref, bf16[64,2048]{1,0:T(8,128)(2,1)S(1)} %copy.24.left_ref, f32[8,64,8]{2,1,0:T(8,128)S(1)} %bitcast.34, ...), custom_call_target="tpu_custom_call" | custom-call | tf_op jit(solution)/shard_map/pairs/pallas_call | solution.py:356
  79.3 0.7 copy-done.3
  80.0 0.7 copy-done.5
  80.7 1.5 %reshape.68 = bf16[64,32,64]{2,1,0:T(8,128)(2,1)S(1)} reshape(bf16[4,16,2048]{2,1,0:T(8,128)(2,1)} %copy-done.5) | data formatting | bytes 524288 | tf_op jit(solution)/shard_map/reshape | solution.py:557
  82.2 1.3 %copy.27 = bf16[64,32,64]{1,2,0:T(8,128)(2,1)} copy(bf16[64,32,64]{2,1,0:T(8,128)(2,1)S(1)} %reshape.68) | data formatting | bytes 524288 | tf_op jit(solution)/shard_map/reshape | solution.py:557
  83.6 0.8 concatenate.11
  84.4 1.8 %pad_maximum_fusion.grads_ref = bf16[4096,64]{1,0:T(8,128)(2,1)S(1)} fusion(bf16[4096,32]{1,0:T(8,128)(2,1)} %bitcast.35, bf16[4096,32]{1,0:T(8,128)(2,1)S(1)} %concatenate.11), kind=kLoop, calls=%fused_computation.15 | loop fusion | flops 1048576 | bytes 1048576 | tf_op jit(solution)/shard_map/concatenate | solution.py:558
  86.2 6.9 %tail.1 = (bf16[4096,256]{1,0:T(8,128)(2,1)S(1)}, f32[256,32]{1,0:T(8,128)S(1)}, f32[256,32]{1,0:T(8,128)S(1)}) custom-call(bf16[4096,256]{1,0:T(8,128)(2,1)S(1)} %bitcast.30, bf16[4096,64]{1,0:T(8,128)(2,1)S(1)} %pad_maximum_fusion.grads_ref, bf16[256,64]{1,0:T(8,128)(2,1)S(1)} %pad_maximum_fusion.1.weights_ref), custom_call_target="tpu_custom_call" | custom-call | tf_op jit(solution)/shard_map/tail/pallas_call | solution.py:489
  93.1 1.3 %copy-done.1 = bf16[4096,256]{1,0:T(8,128)(2,1)} copy-done((bf16[4096,256]{1,0:T(8,128)(2,1)}, bf16[4096,256]{1,0:T(8,128)(2,1)S(1)}, u32[]{:S(2)}) %copy-start.1) | copy-done | bytes 2097176
  94.4 0.7 copy.30
  95.1 0.7 copy.31
  95.8 1.0 copy.40
  96.8 1.3 %copy.41 = bf16[64,64,256]{2,1,0:T(8,128)(2,1)} copy(bf16[64,64,256]{2,1,0:T(8,128)(2,1)S(1)} %bitcast.33) | data formatting | bytes 4194304
  98.1 0.6 copy.42
  (33 shorter events, 0.4 us)
Async XLA Ops:
  0.6 2.4 %copy-start = (bf16[64,64,256]{2,1,0:T(8,128)(2,1)S(1)}, bf16[64,64,256]{2,1,0:T(8,128)(2,1)}, u32[]{:S(2)}) copy-start(bf16[64,64,256]{2,1,0:T(8,128)(2,1)} %param.7) | copy-start | bytes 6291460
  0.6 3.7 %copy-start.10 = (s32[64,256]{1,0:T(8,128)S(1)}, s32[64,256]{1,0:T(8,128)}, u32[]{:S(2)}) copy-start(s32[64,256]{1,0:T(8,128)} %param.8) | copy-start | bytes 196612
  0.7 3.7 %copy-start.14 = (s32[256]{0:T(256)S(1)}, s32[256]{0:T(256)}, u32[]{:S(2)}) copy-start(s32[256]{0:T(256)} %param.9) | copy-start | bytes 3076
  0.7 5.4 %copy-start.11 = (bf16[256,32]{0,1:T(8,128)(2,1)S(1)}, bf16[256,32]{0,1:T(8,128)(2,1)}, u32[]{:S(2)}) copy-start(bf16[256,32]{0,1:T(8,128)(2,1)} %param.10) | copy-start | bytes 49156
  0.7 5.6 %copy-start.12 = (bf16[256,32]{0,1:T(8,128)(2,1)S(1)}, bf16[256,32]{0,1:T(8,128)(2,1)}, u32[]{:S(2)}) copy-start(bf16[256,32]{0,1:T(8,128)(2,1)} %param.11) | copy-start | bytes 49156
  3.0 3.6 %copy-start.7 = (bf16[1024,128]{1,0:T(8,128)(2,1)S(1)}, bf16[1024,128]{1,0:T(8,128)(2,1)}, u32[]{:S(2)}) copy-start(bf16[1024,128]{1,0:T(8,128)(2,1)} %param.12) | copy-start | bytes 786436
  5.1 1.7 %copy-start.8 = (f32[64,64]{1,0:T(8,128)}, f32[64,64]{1,0:T(8,128)S(1)}, u32[]{:S(2)}) copy-start(f32[64,64]{1,0:T(8,128)S(1)} %get-tuple-element.30) | copy-start | bytes 49156
  6.9 3.1 %copy-start.9 = (f32[64,64]{1,0:T(8,128)S(1)}, f32[64,64]{1,0:T(8,128)}, u32[]{:S(2)}) copy-start(f32[64,64]{1,0:T(8,128)} %copy-done.8) | copy-start | bytes 49156
  10.0 5.5 %copy-start.13 = (bf16[256,32]{0,1:T(8,128)(2,1)S(1)}, bf16[256,32]{0,1:T(8,128)(2,1)}, u32[]{:S(2)}) copy-start(bf16[256,32]{0,1:T(8,128)(2,1)} %param.11) | copy-start | bytes 49156
  79.3 0.7 copy-start.3
  80.0 0.7 copy-start.5
  80.7 2.9 %copy-start.4 = (bf16[4,16,2048]{2,1,0:T(8,128)(2,1)S(1)}, bf16[4,16,2048]{2,1,0:T(8,128)(2,1)}, u32[]{:S(2)}) copy-start(bf16[4,16,2048]{2,1,0:T(8,128)(2,1)} %copy-done.3) | copy-start | bytes 786436
  86.2 9.6 %copy-start.6 = (bf16[64,64,128]{2,1,0:T(8,128)(2,1)S(1)}, bf16[64,64,128]{2,1,0:T(8,128)(2,1)}, u32[]{:S(2)}) copy-start(bf16[64,64,128]{2,1,0:T(8,128)(2,1)} %get-tuple-element.39) | copy-start | bytes 3145732
  93.1 1.3 %copy-start.1 = (bf16[4096,256]{1,0:T(8,128)(2,1)}, bf16[4096,256]{1,0:T(8,128)(2,1)S(1)}, u32[]{:S(2)}) copy-start(bf16[4096,256]{1,0:T(8,128)(2,1)S(1)} %get-tuple-element.15) | copy-start | bytes 6291460
  94.4 2.4 %copy-start.2 = (bf16[4096,256]{1,0:T(8,128)(2,1)S(1)}, bf16[4096,256]{1,0:T(8,128)(2,1)}, u32[]{:S(2)}) copy-start(bf16[4096,256]{1,0:T(8,128)(2,1)} %copy-done.1) | copy-start | bytes 6291460

commit v3 on v2

--- a/solution.py
+++ b/solution.py
@@ -37,8 +37,6 @@
     cot_ref,
     wst_ref,
     wst2_ref,
-    live_left_ref,
-    live_right_ref,
     pair_ref,
     out_l,
     out_r,
@@ -152,10 +150,29 @@
                 right_ref[:, at : at + residues] = got[k, :, e * residues : (e + 1) * residues]
 
     wide = 256
+    slab_l = seqs // col_devs
+    for n in range(0, rows * width, wide):
+        gl = lax.dot_general(
+            right_ref[...], gp_ref[n : n + wide], NT, preferred_element_type=f32
+        )
+        gl = gl.astype(bf16)
+        for src in range(col_devs):
+            gl_ref[src, :, n : n + wide] = gl[src * slab_l : (src + 1) * slab_l]
+    lefts = []
+    for d in range(1, col_devs):
+        peer = lax.rem(c + d, col_devs)
+        lefts.append(
+            remote(
+                gl_ref.at[peer], buf_l.at[d - 1], l_send.at[d - 1], l_recv.at[d - 1], {"col": peer}
+            )
+        )
+    for copy in lefts:
+        copy.start()
+
     slab = seqs // row_devs
     for n in range(0, cols * width, wide):
         gr = jnp.dot(left_ref[...], gp_ref[:, n : n + wide], preferred_element_type=f32)
-        gr = (gr * live_right_ref[:, n : n + wide].astype(f32)).astype(bf16)
+        gr = gr.astype(bf16)
         for src in range(row_devs):
             piece = gr[src * slab : (src + 1) * slab]
             if ratio == 1:
@@ -175,42 +192,29 @@
     for copy in rights:
         copy.start()
 
-    slab_l = seqs // col_devs
-    for n in range(0, rows * width, wide):
-        gl = lax.dot_general(
-            right_ref[...], gp_ref[n : n + wide], NT, preferred_element_type=f32
-        )
-        gl = (gl * live_left_ref[:, n : n + wide].astype(f32)).astype(bf16)
-        for src in range(col_devs):
-            gl_ref[src, :, n : n + wide] = gl[src * slab_l : (src + 1) * slab_l]
-    lefts = []
-    for d in range(1, col_devs):
-        peer = lax.rem(c + d, col_devs)
-        lefts.append(
-            remote(
-                gl_ref.at[peer], buf_l.at[d - 1], l_send.at[d - 1], l_recv.at[d - 1], {"col": peer}
-            )
-        )
-    for copy in lefts:
-        copy.start()
-
     gw_acc[...] = jnp.zeros_like(gw_acc)
     lanes = lax.broadcasted_iota(jnp.int32, (z, tile), 1)
 
-    def pair_step(b, carry):
+    def outer_step(b, carry):
         left = left_ref[:, pl.ds(pl.multiple_of(b * (ib * width), ib * width), ib * width)]
+        at = pl.ds(pl.multiple_of(b * (ib * tile), ib * tile), ib * tile)
         for g in range(groups):
             part = lax.dot_general(
                 left, right_ref[:, g * tile : (g + 1) * tile], TN, preferred_element_type=f32
             ).astype(bf16)
             for i in range(ib):
-                x_ref[g * width : (g + 1) * width, i * tile : (i + 1) * tile] = part[
+                x_ref[b, g * width : (g + 1) * width, i * tile : (i + 1) * tile] = part[
                     i * width : (i + 1) * width
                 ]
+        share = jnp.dot(x_ref[b], s_ref[at], preferred_element_type=f32)
+        gw_acc[...] += share.reshape(groups, width, per * z)
+        return carry
+
+    def pair_step(b, carry):
         inverse = 1.0 / div_ref[b]
         for i in range(ib):
             sl = slice(i * tile, (i + 1) * tile)
-            y = jnp.dot(wst_ref[...], x_ref[:, sl], preferred_element_type=f32)
+            y = jnp.dot(wst_ref[...], x_ref[b, :, sl], preferred_element_type=f32)
             picked = y[:z]
             for p in range(1, per):
                 picked = jnp.where(lanes < p * cols, picked, y[p * z : (p + 1) * z])
@@ -219,12 +223,9 @@
             for p in range(1, per):
                 total = total + turned[p * cols : (p + 1) * cols]
             pair_ref[b * ib + i] = (total * inverse[:, i : i + 1]).astype(bf16)
-        block = s_ref[pl.ds(pl.multiple_of(b * (ib * tile), ib * tile), ib * tile)]
-        share = jnp.dot(x_ref[...], block, preferred_element_type=f32)
-        gw_acc[...] += share.reshape(groups, width, per * z)
         return carry
 
-    lax.fori_loop(0, steps // 2, pair_step, 0)
+    lax.fori_loop(0, steps // 2, outer_step, 0)
 
     for copy in rights:
         copy.wait_recv()
@@ -270,7 +271,7 @@
         copy.start()
     out_l[c] = done_l[...]
 
-    lax.fori_loop(steps // 2, steps, pair_step, 0)
+    lax.fori_loop(steps // 2, steps, outer_step, 0)
 
     chunk = out_w.shape[0]
     piece = min(groups, chunk)
@@ -290,6 +291,8 @@
     for copy in outs:
         copy.start()
 
+    lax.fori_loop(0, steps, pair_step, 0)
+
     for copy in left_copies:
         copy.wait_recv()
     for src in range(row_devs):
@@ -333,7 +336,7 @@
 
 
 def pairs(
-    own, left, divisor, cotangent, weight, live_left, live_right, width, row_devs, col_devs, scale
+    own, left, divisor, cotangent, weight, width, row_devs, col_devs, scale
 ):
     rows, cols, z = cotangent.shape
     seqs = left.shape[0]
@@ -361,12 +364,12 @@
             jax.ShapeDtypeStruct((row_devs,) + r_shape, bf16),
             jax.ShapeDtypeStruct((chunk, z), f32),
         ),
-        in_specs=[VMEM] * 8,
+        in_specs=[VMEM] * 6,
         out_specs=(VMEM,) * 4,
         scratch_shapes=[
             vmem((ratio, seqs, residues * width), bf16),
             vmem((seqs, cols * width), bf16),
-            vmem((groups * width, ib * tile), bf16),
+            vmem((steps, groups * width, ib * tile), bf16),
             vmem((rows * tile, per * z), bf16),
             vmem((rows * width, groups * tile), bf16),
             vmem((groups, width, per * z), f32),
@@ -395,18 +398,16 @@
             collective_id=0, has_side_effects=True, vmem_limit_bytes=52 * 1024 * 1024
         ),
         name="pairs",
-    )(own, left, div, cotangent, wst2.T, wst2, live_left, live_right)
+    )(own, left, div, cotangent, wst2.T, wst2)
 
 
 def tail_kernel(
     row_devs,
-    scale,
     x_ref,
     grads_ref,
     weights_ref,
     align_ref,
-    left_ref,
-    right_ref,
+    out_ref,
     buf,
     unit_ref,
     inv_ref,
@@ -474,27 +475,22 @@
     total = buf[0]
     for src in range(1, row_devs):
         total = total + buf[src]
-    total = (total * scale).T
-    width = left_ref.shape[1]
-    left_ref[...] = total[:, :width]
-    right_ref[...] = total[:, width:]
+    out_ref[...] = total
     for copy in copies:
         copy.wait_send()
 
 
-def tail(x, grads, weights, row_devs, scale):
+def tail(x, grads, weights, row_devs):
     rows, channels = x.shape
     both = grads.shape[1]
-    width = both // 2
     return pl.pallas_call(
-        functools.partial(tail_kernel, row_devs, scale),
+        functools.partial(tail_kernel, row_devs),
         out_shape=(
             jax.ShapeDtypeStruct(x.shape, bf16),
-            jax.ShapeDtypeStruct((channels, width), f32),
-            jax.ShapeDtypeStruct((channels, width), f32),
+            jax.ShapeDtypeStruct((both, channels), f32),
         ),
         in_specs=[VMEM] * 3,
-        out_specs=(VMEM,) * 3,
+        out_specs=(VMEM,) * 2,
         scratch_shapes=[
             pltpu.VMEM((row_devs, both, channels), f32),
             pltpu.VMEM((rows, channels), f32),
@@ -537,8 +533,6 @@
     left = jnp.einsum("snd,dc->snc", normed, left_weight, preferred_element_type=f32)
     left = (left * own_live[..., None]).astype(bf16).reshape(seqs, residues * width)
     divisor = jnp.maximum(jnp.dot(own_live.T, live_cols, precision=lax.Precision.HIGHEST), 1.0)
-    live_left = jnp.repeat(own_live.astype(bf16), width, axis=1)
-    live_right = jnp.tile(live_cols.astype(bf16), (1, width))
 
     pair, grad_left, grad_right, out_share = pairs(
         right_own,
@@ -546,8 +540,6 @@
         divisor,
         cotangent,
         output_weight,
-        live_left,
-        live_right,
         width,
         row_devs,
         col_devs,
@@ -555,10 +547,13 @@
     )
     grad_left = grad_left.reshape(seqs, residues, width)
     grad_right = grad_right.reshape(seqs, width, residues).transpose(0, 2, 1)
-    grads = jnp.concatenate([grad_left, grad_right], -1).reshape(seqs * residues, 2 * width)
+    grads = jnp.concatenate([grad_left, grad_right], -1) * own_live.astype(bf16)[..., None]
+    grads = grads.reshape(seqs * residues, 2 * width)
     weights = jnp.concatenate([left_weight, right_weight], -1)
     flat = alignment_activations.reshape(seqs * residues, channels)
-    align, left_wgrad, right_wgrad = tail(flat, grads, weights, row_devs, 1.0 / residue_total)
+    align, wgrad = tail(flat, grads, weights, row_devs)
+    left_wgrad = wgrad[:width].T / residue_total
+    right_wgrad = wgrad[width:].T / residue_total
     align = align.reshape(seqs, residues, channels)
     return (pair, align, out_share, left_wgrad, right_wgrad)
 

time: 99.3 us -> 92.6 us (0.933)
  local copies, waits for them, and re-layouts: 19.7 us -> 13.4 us
  Pallas kernels: 66.2 us -> 65 us
    unnamed x38 -> x26, local copies, waits for them, and re-layouts: 7.32 us -> 4.61 us
    mul x0 -> x1, other arithmetic: none -> 2.03 us  [body(): jnp.concatenate([grad_left, grad_right], -1)]
    pallas_call x1, Pallas kernels: 59.3 us -> 57.5 us  [pairs(): pl.pallas_call(functools.partial(pairs_kernel, row_devs, col_devs, ib, wi...]
    concatenate x1 -> x0, other arithmetic: 1.81 us -> none  [body(): jnp.concatenate([grad_left, grad_right], -1)]
    another operation x2 -> x0, local copies, waits for them, and re-layouts: 1.26 us -> none  [body(): live_right = jnp.tile(live_cols.astype(bf16), (1, width))]
where the time goes in v3:
time: 92.6 us; the launch traced here: 92 us
  Pallas kernels  65 us (70%)
  local copies, waits for them, and re-layouts  13.4 us (14%)
  other arithmetic  7.06 us (8%)
  matrix products  5.71 us (6%)
    pallas_call x1, Pallas kernels, pairs(): pl.pallas_call(functools.partial(pairs_kernel, row_devs, col_devs, ib, wi...  57.5 us
    pallas_call x1, Pallas kernels, tail(): pl.pallas_call(functools.partial(tail_kernel, row_devs), out_shape=(jax.S...  7.48 us
    unnamed x26, local copies, waits for them, and re-layouts  4.61 us
    dot_general x1, matrix products, body(): jnp.einsum('snd,de->sen', normed, right_weight, preferred_element_type=f32)  3.07 us
    reshape x2, local copies, waits for them, and re-layouts, body(): grad_right = grad_right.reshape(seqs, width, residues).transpose(0, 2, 1)  2.85 us
    dot_general x1, matrix products, body(): jnp.einsum('snd,dc->snc', normed, left_weight, preferred_element_type=f32)  2.38 us
    reduce_sum x1, other arithmetic, layer_normalize(): average = jnp.mean(floats, -1, keepdims=True)  2.35 us
    mul x1, other arithmetic, body(): jnp.concatenate([grad_left, grad_right], -1)  2.03 us

profile of v3, /device:TPU:0, one launch (start us, length us, event | category | flops | bytes accessed | tf_op | source)
XLA Modules:
  0.0 92.0 jit_solution(5392104819194146482)
XLA Ops:
  0.7 0.0 copy-start.7
  0.7 0.0 copy-start.8
  0.7 2.3 %convert_reduce_fusion = f32[64,64]{1,0:T(8,128)S(1)} fusion(bf16[64,64,256]{2,1,0:T(8,128)(2,1)} %param.7), kind=kLoop, calls=%fused_computation.1 | loop fusion | flops 2093056 | bytes 2113536 | tf_op jit(solution)/shard_map/reduce_sum | solution.py:21
  3.0 0.0 copy-start.5
  3.1 1.3 %fusion.2 = f32[64,64]{1,0:T(8,128)S(1)} fusion(bf16[64,64,256]{2,1,0:T(8,128)(2,1)S(1)} %copy-done, f32[64,64]{1,0:T(8,128)S(1)} %broadcast_multiply_fusion), kind=kLoop, calls=%fused_computation.4 | loop fusion | flops 4190208 | bytes 2129920 | tf_op jit(solution)/shard_map/reduce_sum | solution.py:23
  4.4 0.6 fusion.29
  5.1 0.3 fusion.23
  5.3 0.1 mul.61
  5.4 0.1 copy.24
  5.5 0.1 copy.25
  5.7 0.1 pad_maximum_fusion.weights_ref
  5.8 0.1 copy.19
  5.9 0.2 copy.20
  6.2 0.1 copy.22.wst_ref
  6.3 2.4 %fusion.14 = bf16[64,64,32]{1,2,0:T(8,128)(2,1)S(1)} fusion(bf16[64,64,256]{2,1,0:T(8,128)(2,1)S(1)} %copy-done, f32[64,64]{1,0:T(8,128)} %get-tuple-element.23, f32[64,64]{1,0:T(8,128)S(1)} %broadcast_multiply_fusion, f32[64,64]{1,0:T(8,128)S(1)} %get-tuple-element.18, bf16[256,32]{0,1:T(8,128)(2,1)} %param.10), kind=kOutput, calls=%fused_computation.10 | convolution fusion | flops 71565312 | bytes 2424832 | tf_op jit(solution)/shard_map/snd,dc->snc/dot_general | solution.py:533
  8.7 1.8 %copy.18 = bf16[64,64,32]{0,2,1:T(8,128)(2,1)} copy(bf16[64,64,32]{1,2,0:T(8,128)(2,1)S(1)} %fusion.14) | data formatting | bytes 524288 | tf_op jit(solution)/shard_map/convert_element_type | solution.py:534
  10.6 1.2 %copy.21.left_ref = bf16[64,2048]{1,0:T(8,128)(2,1)S(1)} copy(bf16[64,2048]{0,1:T(8,128)(2,1)} %bitcast.39) | data formatting | bytes 524288 | tf_op jit(solution)/shard_map/reshape | solution.py:534
  11.8 3.1 %fusion.20 = bf16[64,32,64]{2,1,0:T(8,128)(2,1)} fusion(bf16[64,64,256]{2,1,0:T(8,128)(2,1)S(1)} %copy-done, f32[64,64]{1,0:T(8,128)} %get-tuple-element.23, f32[64,64]{1,0:T(8,128)S(1)} %broadcast_multiply_fusion, f32[64,64]{1,0:T(8,128)S(1)} %get-tuple-element.18, bf16[256,32]{0,1:T(8,128)(2,1)} %param.11), kind=kOutput, calls=%fused_computation.12 | convolution fusion | flops 71565312 | bytes 2424832 | tf_op jit(solution)/shard_map/snd,de->sen/dot_general | solution.py:531
  14.9 1.5 %reshape.57.own_ref = bf16[64,2048]{1,0:T(8,128)(2,1)S(1)} reshape(bf16[64,32,64]{2,1,0:T(8,128)(2,1)} %fusion.20) | data formatting | bytes 524288 | tf_op jit(solution)/shard_map/reshape | solution.py:532
  16.4 57.5 %pairs.1 = (bf16[64,64,128]{2,1,0:T(8,128)(2,1)}, bf16[4,16,2048]{2,1,0:T(8,128)(2,1)S(1)}, bf16[4,16,2048]{2,1,0:T(8,128)(2,1)S(1)}, f32[64,128]{1,0:T(8,128)S(1)}) custom-call(bf16[64,2048]{1,0:T(8,128)(2,1)S(1)} %reshape.57.own_ref, bf16[64,2048]{1,0:T(8,128)(2,1)S(1)} %copy.21.left_ref, f32[8,64,8]{2,1,0:T(8,128)S(1)} %bitcast.37, ...), custom_call_target="tpu_custom_call" | custom-call | tf_op jit(solution)/shard_map/pairs/pallas_call | solution.py:359
  73.8 0.0 copy-start.1
  73.9 0.7 copy-done.1
  74.6 0.7 copy-done.3
  75.3 1.5 %reshape.63 = bf16[64,32,64]{2,1,0:T(8,128)(2,1)S(1)} reshape(bf16[4,16,2048]{2,1,0:T(8,128)(2,1)} %copy-done.3) | data formatting | bytes 524288 | tf_op jit(solution)/shard_map/reshape | solution.py:549
  76.8 1.3 %copy.23 = bf16[64,32,64]{1,2,0:T(8,128)(2,1)} copy(bf16[64,32,64]{2,1,0:T(8,128)(2,1)S(1)} %reshape.63) | data formatting | bytes 524288 | tf_op jit(solution)/shard_map/reshape | solution.py:549
  78.1 0.8 concatenate.11
  78.9 2.0 %maximum_multiply_fusion.grads_ref = bf16[4096,64]{1,0:T(8,128)(2,1)S(1)} fusion(bf16[4096,32]{1,0:T(8,128)(2,1)} %bitcast.38, bf16[4096,32]{1,0:T(8,128)(2,1)S(1)} %concatenate.11, bf16[4096]{0:T(1024)(128)(2,1)S(1)} %mul.61), kind=kLoop, calls=%fused_computation.15 | loop fusion | flops 1572864 | bytes 1056768 | tf_op jit(solution)/shard_map/mul | solution.py:550
  81.0 7.5 %tail.1 = (bf16[4096,256]{1,0:T(8,128)(2,1)S(1)}, f32[64,256]{1,0:T(8,128)S(1)}) custom-call(bf16[4096,256]{1,0:T(8,128)(2,1)S(1)} %bitcast.33, bf16[4096,64]{1,0:T(8,128)(2,1)S(1)} %maximum_multiply_fusion.grads_ref, bf16[256,64]{1,0:T(8,128)(2,1)S(1)} %pad_maximum_fusion.weights_ref), custom_call_target="tpu_custom_call" | custom-call | tf_op jit(solution)/shard_map/tail/pallas_call | solution.py:486
  88.5 0.6 multiply_bitcast_fusion
  89.1 1.0 %copy.34 = bf16[64,64,128]{2,1,0:T(8,128)(2,1)} copy(bf16[64,64,128]{2,1,0:T(8,128)(2,1)S(1)} %copy-done.4) | data formatting | bytes 2097152
  90.1 1.3 %copy.35 = bf16[64,64,256]{2,1,0:T(8,128)(2,1)} copy(bf16[64,64,256]{2,1,0:T(8,128)(2,1)S(1)} %bitcast.36) | data formatting | bytes 4194304
  91.4 0.6 copy.36
  (17 shorter events, 0.1 us)
Async XLA Ops:
  0.6 2.4 %copy-start = (bf16[64,64,256]{2,1,0:T(8,128)(2,1)S(1)}, bf16[64,64,256]{2,1,0:T(8,128)(2,1)}, u32[]{:S(2)}) copy-start(bf16[64,64,256]{2,1,0:T(8,128)(2,1)} %param.7) | copy-start | bytes 6291460
  0.6 3.7 %copy-start.6 = (s32[64,256]{1,0:T(8,128)S(1)}, s32[64,256]{1,0:T(8,128)}, u32[]{:S(2)}) copy-start(s32[64,256]{1,0:T(8,128)} %param.8) | copy-start | bytes 196612
  0.7 3.7 %copy-start.9 = (s32[256]{0:T(256)S(1)}, s32[256]{0:T(256)}, u32[]{:S(2)}) copy-start(s32[256]{0:T(256)} %param.9) | copy-start | bytes 3076
  0.7 4.8 %copy-start.7 = (bf16[256,32]{0,1:T(8,128)(2,1)S(1)}, bf16[256,32]{0,1:T(8,128)(2,1)}, u32[]{:S(2)}) copy-start(bf16[256,32]{0,1:T(8,128)(2,1)} %param.10) | copy-start | bytes 49156
  0.7 4.9 %copy-start.8 = (bf16[256,32]{0,1:T(8,128)(2,1)S(1)}, bf16[256,32]{0,1:T(8,128)(2,1)}, u32[]{:S(2)}) copy-start(bf16[256,32]{0,1:T(8,128)(2,1)} %param.11) | copy-start | bytes 49156
  3.0 2.9 %copy-start.5 = (bf16[1024,128]{1,0:T(8,128)(2,1)S(1)}, bf16[1024,128]{1,0:T(8,128)(2,1)}, u32[]{:S(2)}) copy-start(bf16[1024,128]{1,0:T(8,128)(2,1)} %param.12) | copy-start | bytes 786436
  73.8 0.7 copy-start.1
  74.6 0.7 copy-start.3
  75.3 2.9 %copy-start.2 = (bf16[4,16,2048]{2,1,0:T(8,128)(2,1)S(1)}, bf16[4,16,2048]{2,1,0:T(8,128)(2,1)}, u32[]{:S(2)}) copy-start(bf16[4,16,2048]{2,1,0:T(8,128)(2,1)} %copy-done.1) | copy-start | bytes 786436
  81.0 8.1 %copy-start.4 = (bf16[64,64,128]{2,1,0:T(8,128)(2,1)S(1)}, bf16[64,64,128]{2,1,0:T(8,128)(2,1)}, u32[]{:S(2)}) copy-start(bf16[64,64,128]{2,1,0:T(8,128)(2,1)} %get-tuple-element.29) | copy-start | bytes 3145732

commit v4 on v3

--- a/solution.py
+++ b/solution.py
@@ -53,6 +53,8 @@
     buf_l,
     buf_r,
     buf_w,
+    buf_v,
+    done_w,
     done_l,
     done_r,
     a_send,
@@ -63,6 +65,8 @@
     r_recv,
     w_send,
     w_recv,
+    v_send,
+    v_recv,
     l2_send,
     l2_recv,
     r2_send,
@@ -283,15 +287,35 @@
                 at = flat % chunk
                 gw_ref[flat // chunk, at : at + piece] = row[o : o + piece, p * z : (p + 1) * z]
     outs = []
-    for d in range(1, count):
-        peer, where = place(d)
+    for d in range(1, row_devs):
+        peer = lax.rem(r + d, row_devs)
+        part = gw_ref.at[pl.ds(peer * col_devs, col_devs)]
         outs.append(
-            remote(gw_ref.at[peer], buf_w.at[d - 1], w_send.at[d - 1], w_recv.at[d - 1], where)
+            remote(part, buf_w.at[d - 1], w_send.at[d - 1], w_recv.at[d - 1], {"row": peer})
         )
     for copy in outs:
         copy.start()
 
-    lax.fori_loop(0, steps, pair_step, 0)
+    lax.fori_loop(0, steps // 2, pair_step, 0)
+
+    for copy in outs:
+        copy.wait_recv()
+    total = gw_ref[pl.ds(r * col_devs, col_devs)].astype(f32)
+    for d in range(1, row_devs):
+        total = total + buf_w[d - 1].astype(f32)
+    done_w[...] = total.astype(bf16)
+    out_copies = []
+    for d in range(1, col_devs):
+        peer = lax.rem(c + d, col_devs)
+        out_copies.append(
+            remote(
+                done_w.at[peer], buf_v.at[d - 1], v_send.at[d - 1], v_recv.at[d - 1], {"col": peer}
+            )
+        )
+    for copy in out_copies:
+        copy.start()
+
+    lax.fori_loop(steps // 2, steps, pair_step, 0)
 
     for copy in left_copies:
         copy.wait_recv()
@@ -305,11 +329,11 @@
                 done_r.at[0], out_r.at[src], r2_send.at[0], r2_recv.at[src], where
             ).wait_recv()
 
-    for copy in outs:
+    for copy in out_copies:
         copy.wait_recv()
-    total = gw_ref[me].astype(f32)
-    for d in range(1, count):
-        total = total + buf_w[d - 1].astype(f32)
+    total = done_w[c].astype(f32)
+    for d in range(1, col_devs):
+        total = total + buf_v[d - 1].astype(f32)
     total = total * scale
     if per == 1:
         out_w[...] = total
@@ -318,7 +342,7 @@
             ch, p = o // groups // per, o // groups % per
             out_w[pl.ds(ch * width + p, groups, stride=per), :] = total[o : o + groups]
 
-    for copy in rights + lefts + outs + left_copies:
+    for copy in rights + lefts + outs + left_copies + out_copies:
         copy.wait_send()
     for k in range(ratio):
 
@@ -378,7 +402,9 @@
             vmem((count, chunk, z), bf16),
             vmem((col_devs - 1,) + l_shape, bf16),
             vmem((row_devs - 1, ratio) + r_shape, bf16),
-            vmem((count - 1, chunk, z), bf16),
+            vmem((row_devs - 1, col_devs, chunk, z), bf16),
+            vmem((col_devs - 1, chunk, z), bf16),
+            vmem((col_devs, chunk, z), bf16),
             vmem(l_shape, bf16),
             vmem((ratio,) + r_shape, bf16),
             dma((row_devs,)),
@@ -387,8 +413,10 @@
             dma((col_devs - 1,)),
             dma((row_devs - 1,)),
             dma((row_devs - 1,)),
-            dma((count - 1,)),
-            dma((count - 1,)),
+            dma((row_devs - 1,)),
+            dma((row_devs - 1,)),
+            dma((col_devs - 1,)),
+            dma((col_devs - 1,)),
             dma((col_devs - 1,)),
             dma((col_devs - 1,)),
             dma((ratio * col_devs,)),

time: 92.6 us -> 88.2 us (0.952)
  Pallas kernels: 65 us -> 60.5 us
    pallas_call x1, Pallas kernels: 57.5 us -> 52.8 us  [pairs(): pl.pallas_call(functools.partial(pairs_kernel, row_devs, col_devs, ib, wi...]
where the time goes in v4:
time: 88.2 us; the launch traced here: 87.6 us
  Pallas kernels  60.5 us (69%)
  local copies, waits for them, and re-layouts  13.4 us (15%)
  other arithmetic  7.06 us (8%)
  matrix products  5.71 us (6%)
    pallas_call x1, Pallas kernels, pairs(): pl.pallas_call(functools.partial(pairs_kernel, row_devs, col_devs, ib, wi...  52.8 us
    pallas_call x1, Pallas kernels, tail(): pl.pallas_call(functools.partial(tail_kernel, row_devs), out_shape=(jax.S...  7.69 us
    unnamed x26, local copies, waits for them, and re-layouts  4.61 us
    dot_general x1, matrix products, body(): jnp.einsum('snd,de->sen', normed, right_weight, preferred_element_type=f32)  3.07 us
    reshape x2, local copies, waits for them, and re-layouts, body(): grad_right = grad_right.reshape(seqs, width, residues).transpose(0, 2, 1)  2.85 us
    dot_general x1, matrix products, body(): jnp.einsum('snd,dc->snc', normed, left_weight, preferred_element_type=f32)  2.38 us
    reduce_sum x1, other arithmetic, layer_normalize(): average = jnp.mean(floats, -1, keepdims=True)  2.35 us
    mul x1, other arithmetic, body(): jnp.concatenate([grad_left, grad_right], -1)  2.03 us

profile of v4, /device:TPU:0, one launch (start us, length us, event | category | flops | bytes accessed | tf_op | source)
XLA Modules:
  0.0 87.6 jit_solution(1736141826697515166)
XLA Ops:
  0.7 0.0 copy-start.7
  0.7 0.0 copy-start.8
  0.7 2.3 %convert_reduce_fusion = f32[64,64]{1,0:T(8,128)S(1)} fusion(bf16[64,64,256]{2,1,0:T(8,128)(2,1)} %param.7), kind=kLoop, calls=%fused_computation.1 | loop fusion | flops 2093056 | bytes 2113536 | tf_op jit(solution)/shard_map/reduce_sum | solution.py:21
  3.0 0.0 copy-start.5
  3.1 1.3 %fusion.2 = f32[64,64]{1,0:T(8,128)S(1)} fusion(bf16[64,64,256]{2,1,0:T(8,128)(2,1)S(1)} %copy-done, f32[64,64]{1,0:T(8,128)S(1)} %broadcast_multiply_fusion), kind=kLoop, calls=%fused_computation.4 | loop fusion | flops 4190208 | bytes 2129920 | tf_op jit(solution)/shard_map/reduce_sum | solution.py:23
  4.4 0.6 fusion.29
  5.1 0.3 fusion.23
  5.3 0.1 mul.61
  5.4 0.1 copy.24
  5.5 0.1 copy.25
  5.7 0.1 pad_maximum_fusion.weights_ref
  5.8 0.1 copy.19
  5.9 0.2 copy.20
  6.2 0.1 copy.22.wst_ref
  6.3 2.4 %fusion.14 = bf16[64,64,32]{1,2,0:T(8,128)(2,1)S(1)} fusion(bf16[64,64,256]{2,1,0:T(8,128)(2,1)S(1)} %copy-done, f32[64,64]{1,0:T(8,128)} %get-tuple-element.23, f32[64,64]{1,0:T(8,128)S(1)} %broadcast_multiply_fusion, f32[64,64]{1,0:T(8,128)S(1)} %get-tuple-element.18, bf16[256,32]{0,1:T(8,128)(2,1)} %param.10), kind=kOutput, calls=%fused_computation.10 | convolution fusion | flops 71565312 | bytes 2424832 | tf_op jit(solution)/shard_map/snd,dc->snc/dot_general | solution.py:561
  8.7 1.8 %copy.18 = bf16[64,64,32]{0,2,1:T(8,128)(2,1)} copy(bf16[64,64,32]{1,2,0:T(8,128)(2,1)S(1)} %fusion.14) | data formatting | bytes 524288 | tf_op jit(solution)/shard_map/convert_element_type | solution.py:562
  10.6 1.2 %copy.21.left_ref = bf16[64,2048]{1,0:T(8,128)(2,1)S(1)} copy(bf16[64,2048]{0,1:T(8,128)(2,1)} %bitcast.39) | data formatting | bytes 524288 | tf_op jit(solution)/shard_map/reshape | solution.py:562
  11.8 3.1 %fusion.20 = bf16[64,32,64]{2,1,0:T(8,128)(2,1)} fusion(bf16[64,64,256]{2,1,0:T(8,128)(2,1)S(1)} %copy-done, f32[64,64]{1,0:T(8,128)} %get-tuple-element.23, f32[64,64]{1,0:T(8,128)S(1)} %broadcast_multiply_fusion, f32[64,64]{1,0:T(8,128)S(1)} %get-tuple-element.18, bf16[256,32]{0,1:T(8,128)(2,1)} %param.11), kind=kOutput, calls=%fused_computation.12 | convolution fusion | flops 71565312 | bytes 2424832 | tf_op jit(solution)/shard_map/snd,de->sen/dot_general | solution.py:559
  14.9 1.5 %reshape.57.own_ref = bf16[64,2048]{1,0:T(8,128)(2,1)S(1)} reshape(bf16[64,32,64]{2,1,0:T(8,128)(2,1)} %fusion.20) | data formatting | bytes 524288 | tf_op jit(solution)/shard_map/reshape | solution.py:560
  16.4 52.8 %pairs.1 = (bf16[64,64,128]{2,1,0:T(8,128)(2,1)}, bf16[4,16,2048]{2,1,0:T(8,128)(2,1)S(1)}, bf16[4,16,2048]{2,1,0:T(8,128)(2,1)S(1)}, f32[64,128]{1,0:T(8,128)S(1)}) custom-call(bf16[64,2048]{1,0:T(8,128)(2,1)S(1)} %reshape.57.own_ref, bf16[64,2048]{1,0:T(8,128)(2,1)S(1)} %copy.21.left_ref, f32[8,64,8]{2,1,0:T(8,128)S(1)} %bitcast.37, ...), custom_call_target="tpu_custom_call" | custom-call | tf_op jit(solution)/shard_map/pairs/pallas_call | solution.py:383
  69.2 0.0 copy-start.1
  69.2 0.7 copy-done.1
  69.9 0.7 copy-done.3
  70.6 1.5 %reshape.63 = bf16[64,32,64]{2,1,0:T(8,128)(2,1)S(1)} reshape(bf16[4,16,2048]{2,1,0:T(8,128)(2,1)} %copy-done.3) | data formatting | bytes 524288 | tf_op jit(solution)/shard_map/reshape | solution.py:577
  72.1 1.3 %copy.23 = bf16[64,32,64]{1,2,0:T(8,128)(2,1)} copy(bf16[64,32,64]{2,1,0:T(8,128)(2,1)S(1)} %reshape.63) | data formatting | bytes 524288 | tf_op jit(solution)/shard_map/reshape | solution.py:577
  73.5 0.8 concatenate.11
  74.3 2.0 %maximum_multiply_fusion.grads_ref = bf16[4096,64]{1,0:T(8,128)(2,1)S(1)} fusion(bf16[4096,32]{1,0:T(8,128)(2,1)} %bitcast.38, bf16[4096,32]{1,0:T(8,128)(2,1)S(1)} %concatenate.11, bf16[4096]{0:T(1024)(128)(2,1)S(1)} %mul.61), kind=kLoop, calls=%fused_computation.15 | loop fusion | flops 1572864 | bytes 1056768 | tf_op jit(solution)/shard_map/mul | solution.py:578
  76.3 7.7 %tail.1 = (bf16[4096,256]{1,0:T(8,128)(2,1)S(1)}, f32[64,256]{1,0:T(8,128)S(1)}) custom-call(bf16[4096,256]{1,0:T(8,128)(2,1)S(1)} %bitcast.33, bf16[4096,64]{1,0:T(8,128)(2,1)S(1)} %maximum_multiply_fusion.grads_ref, bf16[256,64]{1,0:T(8,128)(2,1)S(1)} %pad_maximum_fusion.weights_ref), custom_call_target="tpu_custom_call" | custom-call | tf_op jit(solution)/shard_map/tail/pallas_call | solution.py:514
  84.0 0.6 multiply_bitcast_fusion
  84.7 1.0 %copy.34 = bf16[64,64,128]{2,1,0:T(8,128)(2,1)} copy(bf16[64,64,128]{2,1,0:T(8,128)(2,1)S(1)} %copy-done.4) | data formatting | bytes 2097152
  85.6 1.3 %copy.35 = bf16[64,64,256]{2,1,0:T(8,128)(2,1)} copy(bf16[64,64,256]{2,1,0:T(8,128)(2,1)S(1)} %bitcast.36) | data formatting | bytes 4194304
  87.0 0.6 copy.36
  (17 shorter events, 0.1 us)
Async XLA Ops:
  0.6 2.4 %copy-start = (bf16[64,64,256]{2,1,0:T(8,128)(2,1)S(1)}, bf16[64,64,256]{2,1,0:T(8,128)(2,1)}, u32[]{:S(2)}) copy-start(bf16[64,64,256]{2,1,0:T(8,128)(2,1)} %param.7) | copy-start | bytes 6291460
  0.6 3.7 %copy-start.6 = (s32[64,256]{1,0:T(8,128)S(1)}, s32[64,256]{1,0:T(8,128)}, u32[]{:S(2)}) copy-start(s32[64,256]{1,0:T(8,128)} %param.8) | copy-start | bytes 196612
  0.7 3.7 %copy-start.9 = (s32[256]{0:T(256)S(1)}, s32[256]{0:T(256)}, u32[]{:S(2)}) copy-start(s32[256]{0:T(256)} %param.9) | copy-start | bytes 3076
  0.7 4.8 %copy-start.7 = (bf16[256,32]{0,1:T(8,128)(2,1)S(1)}, bf16[256,32]{0,1:T(8,128)(2,1)}, u32[]{:S(2)}) copy-start(bf16[256,32]{0,1:T(8,128)(2,1)} %param.10) | copy-start | bytes 49156
  0.7 4.9 %copy-start.8 = (bf16[256,32]{0,1:T(8,128)(2,1)S(1)}, bf16[256,32]{0,1:T(8,128)(2,1)}, u32[]{:S(2)}) copy-start(bf16[256,32]{0,1:T(8,128)(2,1)} %param.11) | copy-start | bytes 49156
  3.0 2.9 %copy-start.5 = (bf16[1024,128]{1,0:T(8,128)(2,1)S(1)}, bf16[1024,128]{1,0:T(8,128)(2,1)}, u32[]{:S(2)}) copy-start(bf16[1024,128]{1,0:T(8,128)(2,1)} %param.12) | copy-start | bytes 786436
  69.2 0.7 copy-start.1
  69.9 0.7 copy-start.3
  70.6 2.9 %copy-start.2 = (bf16[4,16,2048]{2,1,0:T(8,128)(2,1)S(1)}, bf16[4,16,2048]{2,1,0:T(8,128)(2,1)}, u32[]{:S(2)}) copy-start(bf16[4,16,2048]{2,1,0:T(8,128)(2,1)} %copy-done.1) | copy-start | bytes 786436
  76.3 8.3 %copy-start.4 = (bf16[64,64,128]{2,1,0:T(8,128)(2,1)S(1)}, bf16[64,64,128]{2,1,0:T(8,128)(2,1)}, u32[]{:S(2)}) copy-start(bf16[64,64,128]{2,1,0:T(8,128)(2,1)} %get-tuple-element.29) | copy-start | bytes 3145732
